TPU v7x, 32 devices: a whole 2x2x4 slice. The times are simulated.
32 devices in a mesh: dp: 8 (over y, x, core), mp: 4 (over z).
Axes of the slice: x: 2, y: 2, z: 4, core: 2. Of those that a mesh axis runs over, the one named last changes fastest.
Arguments:
- hidden_in: bfloat16 [2, 8, 448, 768], P(None, 'dp', None, 'mp'), may hold values from -6 to 6
- encoder_states: bfloat16 [2, 8, 1500, 768], P(None, 'dp'), may hold values from -6 to 6
- cotangent: bfloat16 [2, 8, 448, 768], P(None, 'dp', None, 'mp'), may hold values from -6 to 6
- self_qkv: bfloat16 [768, 3, 768], P('dp', None, 'mp'), may hold values from -0.21875 to 0.21875
- self_out: bfloat16 [768, 768], P(('mp', 'dp')), may hold values from -1.25 to 1.25
- cross_q: bfloat16 [768, 768], P('dp', 'mp'), may hold values from -0.21875 to 0.21875
- cross_kv: bfloat16 [768, 2, 768], P('dp', None, 'mp'), may hold values from -0.21875 to 0.21875
- cross_out: bfloat16 [768, 768], P(('mp', 'dp')), may hold values from -1.75 to 1.75
- fc_in: bfloat16 [768, 3072], P('dp', 'mp'), may hold values from -0.21875 to 0.21875
- fc_out: bfloat16 [3072, 768], P(('mp', 'dp')), may hold values from -0.109375 to 0.109375
- ln_gain: float32 [4, 768], P(None, 'mp'), may hold values from 0.5 to 1.5
- ln_bias: float32 [4, 768], P(None, 'mp'), may hold values from -1.5 to 1.5
- token_lengths: int32 [2, 8], P(None, 'dp'), may hold values from 1 to 448, as said below
- audio_lengths: int32 [2, 8], P(None, 'dp'), may hold values from 375 to 1500, as said below
- corpus_ids: int32 [2, 8], P(None, 'dp'), may hold values from 0 to 9
- corpus_weights: float32 [10], replicated, may hold values from 0.3 to 3
Outputs:
- layer_out: bfloat16 [2, 8, 448, 768], P(None, 'dp', None, 'mp')
- grad_hidden: float32 [2, 8, 448, 768], P(None, 'dp', None, 'mp')
- grad_encoder: float32 [2, 8, 1500, 768], P(None, 'dp', None, 'mp')
- grad_self_qkv: float32 [768, 3, 768], P('dp', None, 'mp')
- grad_self_out: float32 [768, 768], P(('mp', 'dp'))
- grad_cross_q: float32 [768, 768], P('dp', 'mp')
- grad_cross_kv: float32 [768, 2, 768], P('dp', None, 'mp')
- grad_cross_out: float32 [768, 768], P(('mp', 'dp'))
- grad_fc_in: float32 [768, 3072], P('dp', 'mp')
- grad_fc_out: float32 [3072, 768], P(('mp', 'dp'))
- grad_ln_gain: float32 [4, 768], P(None, ('mp', 'dp'))
- grad_ln_bias: float32 [4, 768], P(None, ('mp', 'dp'))
Inputs may be any that keep to these rules, and one draw needn't show every extreme that they name: `token_lengths`: each micro-batch's lengths are independent; some sequence of every draw has all 448 tokens live. `audio_lengths`: some sequence of every draw has all 1500 frames live.
All inputs are finite; a program needn't handle non-finite values.
Results may differ from a plain program's by a relative error of at most 0.017.
Values may be sent and summed in bfloat16 or wider, within the bound.
No kernel may reach another device: no remote copies, remote signals or barrier semaphores. Data moves between devices by JAX's collectives and lax.ppermute only.
A program may use at most 192 MiB of HBM per device.

v0:
```python
from functools import partial

import jax
import jax.numpy as jnp
from jax import lax
from jax.experimental import pallas as pl
from jax.experimental.pallas import tpu as pltpu
from jax.sharding import Mesh, PartitionSpec as P

D = 768
HALF = 384
QUARTER = 192
HEAD_DIM = 64
HEADS = 6
CHUNK = 256
BF = jnp.bfloat16
F32 = jnp.float32
AXES = ("xy", "core", "mp")
CHIPS = ("xy", "mp")
VMEM = pl.BlockSpec(memory_space=pltpu.VMEM)
SMEM = pl.BlockSpec(memory_space=pltpu.SMEM)
ANY = pl.BlockSpec(memory_space=pl.ANY)


def mm(left, right):
    return jnp.dot(left, right, preferred_element_type=F32)


def mm_t(left, right):
    return lax.dot_general(left, right, (((1,), (1,)), ((), ())), preferred_element_type=F32)


def shaped(shape, dtype=BF):
    return jax.ShapeDtypeStruct(shape, dtype)


def room(shape, dtype):
    item = jnp.dtype(dtype).itemsize
    shape = (1, 1) + tuple(shape)
    tile = 32 // item
    size = item * (-(-shape[-1] // 128) * 128) * (-(-shape[-2] // tile) * tile)
    for extent in shape[:-2]:
        size *= extent
    return size


def run(
    body, outs, vmem=(), hbm=(), smem=(), scratch=(), copies=0, micros=2, after=(), staged=False
):
    args = tuple(smem) + tuple(vmem) + tuple(hbm)
    count = len(args)
    scratch = list(scratch)
    if copies:
        scratch.append(pltpu.SemaphoreType.DMA((copies,)))
    need = sum(room(a.shape, a.dtype) for a in tuple(vmem) + tuple(outs))
    need += sum(room(a.shape, a.dtype) for a in scratch if a.memory_space == pltpu.VMEM)
    need = min(need + 12 * 1024 * 1024, 60 * 1024 * 1024)
    moved = sum(a.size * a.dtype.itemsize for a in args) + sum(
        o.size * o.dtype.itemsize for o in outs
    )
    skip = len(scratch)
    if staged:
        scratch += [pltpu.VMEM(a.shape, a.dtype) for a in vmem]
        scratch.append(pltpu.SemaphoreType.DMA((len(vmem),)))

    def whole(*refs):
        ins, rest = list(refs[:count]), refs[count + len(after) :]
        if staged:
            held = rest[len(outs) + skip : -1]
            rest, sems = rest[: len(outs) + skip], rest[-1]
            copies = Copies(sems)
            for i, target in enumerate(held):
                copies.start(ins[len(smem) + i], target)
                ins[len(smem) + i] = target
            copies.wait()
        body(*ins, *rest)

    place = ANY if staged else VMEM
    return pl.pallas_call(
        whole,
        out_shape=tuple(outs),
        in_specs=[SMEM] * len(smem) + [place] * len(vmem) + [ANY] * (len(hbm) + len(after)),
        out_specs=(VMEM,) * len(outs),
        scratch_shapes=scratch,
        compiler_params=pltpu.CompilerParams(vmem_limit_bytes=need),
        cost_estimate=pl.CostEstimate(
            flops=int(micros * 1.15e9), bytes_accessed=moved, transcendentals=0
        ),
    )(*args, *after)


class Copies:
    def __init__(self, sems):
        self.sems, self.open = sems, []

    def start(self, source, target):
        copy = pltpu.make_async_copy(source, target, self.sems.at[len(self.open)])
        copy.start()
        self.open.append(copy)

    def wait(self):
        for copy in self.open:
            copy.wait()


def where_am_i():
    return lax.axis_index("core"), lax.axis_index("xy"), lax.axis_index("mp")


class Place:
    def __init__(self, dp, mp):
        self.dp, self.mp = dp, mp
        self.chips = dp // 2
        self.fast = self.chips == 4
        self.z = lax.axis_index("mp")
        self.core = lax.axis_index("core")
        self.xy = lax.axis_index("xy")
        self.d = 2 * self.xy + self.core
        self.micro = self.z % 2
        self.home = self.z // 2

    def move(self, value, route):
        pairs = []
        for xy in range(self.chips):
            for core in range(2):
                for z in range(self.mp):
                    target = route(xy, core, z)
                    if target is not None:
                        txy, tcore, tz = target
                        pairs.append(
                            ((2 * xy + core) * self.mp + z, (2 * txy + tcore) * self.mp + tz)
                        )
        return lax.ppermute(value, AXES, pairs)

    def swap_core(self, value):
        return self.move(value, lambda xy, core, z: (xy, 1 - core, z))

    def swap_xy(self, value, bit):
        return self.move(value, lambda xy, core, z: (xy ^ bit, core, z))

    def swap_z(self, value, bit):
        return self.move(value, lambda xy, core, z: (xy, core, z ^ bit))

    def column_routes(self):
        def route(step, xy, core, z):
            user, j = z // 2, z % 2
            home = core == user
            near = lambda i: (xy, user, 2 * user + i)
            far = lambda i: (xy, user, 2 * (1 - user) + i)
            if step == 0:
                return near(1 - j) if home else far(1 - j)
            if step == 1:
                return far(j) if home else near(j)
            if step == 2:
                return far(1 - j) if home else near(1 - j)
            return None if home else far(j)

        return [partial(route, step) for step in range(4)]

    def column_out(self, shard):
        return [self.move(shard, route) for route in self.column_routes()]

    def column_back(self, blocks):
        got = []
        for block, route in zip(blocks, self.column_routes()):
            turned = {}
            for xy in range(self.chips):
                for core in range(2):
                    for z in range(self.mp):
                        target = route(xy, core, z)
                        if target is not None:
                            turned[target] = (xy, core, z)
            got.append(self.move(block, lambda xy, core, z: turned.get((xy, core, z))))
        return got

    def rows_in(self, blocks):
        def route(k, xy, core, z):
            target = (xy, z // 2, 2 * core + (z + k) % 2)
            return None if target == (xy, core, z) else target

        got = [self.move(block, partial(route, k)) for k, block in enumerate(blocks)]
        return jnp.stack([jnp.where(self.core == self.home, blocks[0], got[0]), got[1]])

    def rows_home(self, blocks):
        return self.rows_joined(blocks, self.rows_sent(blocks))

    def rows_sent(self, blocks):
        def route(k, xy, core, z):
            target = (xy, z // 2, 2 * core + (z % 2 - k) % 2)
            return None if target == (xy, core, z) else target

        return [self.move(block, partial(route, k)) for k, block in enumerate(blocks)]

    def rows_joined(self, blocks, got):
        got = [jnp.where(self.core == self.home, blocks[0], got[0]), got[1]]
        even = self.z % 2 == 0
        both = jnp.stack([jnp.where(even, got[0], got[1]), jnp.where(even, got[1], got[0])])
        return both[:, None].transpose(0, 1, 3, 2)


def norm(hidden):
    center = jnp.mean(hidden, axis=-1, keepdims=True)
    spread = jnp.mean(hidden * hidden, axis=-1, keepdims=True) - center * center
    inverse = lax.rsqrt(spread + 1e-05)
    return (hidden - center) * inverse, inverse


def norm_back(grad, unit, inverse, gain):
    scaled = grad * gain
    first = jnp.mean(scaled, axis=-1, keepdims=True)
    second = jnp.mean(scaled * unit, axis=-1, keepdims=True)
    terms = jnp.concatenate(
        [jnp.sum(grad * unit, axis=0, keepdims=True), jnp.sum(grad, axis=0, keepdims=True)], axis=0
    )
    return inverse * (scaled - first - unit * second), terms


def add_up(*terms):
    total = terms[0].astype(F32)
    for term in terms[1:]:
        total = total + term.astype(F32)
    return total


def input_blocks(hidden, terms, numbers, after=()):
    _, width, length = hidden.shape
    total = width + 32

    def body(numbers_ref, hidden_ref, terms_ref, *outs):
        _, _, z = where_am_i()
        lanes = lax.broadcasted_iota(jnp.int32, (8, length), 1)
        for k in range(2):
            micro = (z + k) % 2
            outs[k][0:width] = hidden_ref[micro]
            tok, aud = numbers_ref[0, micro], numbers_ref[1, micro]
            row = jnp.where(lanes == 0, tok // 256, jnp.where(lanes == 1, tok % 256, 0))
            row = jnp.where(lanes == 2, aud // 256, jnp.where(lanes == 3, aud % 256, row))
            row = jnp.where(lanes == 4, numbers_ref[2, micro], row)
            wide = jnp.concatenate(
                [terms_ref[...].astype(F32), jnp.zeros((24, length - width), F32)], axis=1
            )
            outs[k][width:total] = jnp.concatenate([wide, row.astype(F32)], axis=0).astype(BF)

    return run(
        body,
        [shaped((total, length))] * 2,
        smem=[numbers],
        vmem=[hidden, terms],
        micros=1,
        after=after,
    )


def turned_blocks(value, after=()):
    _, width, length = value.shape

    def body(ref, first_ref, second_ref):
        _, _, z = where_am_i()
        first_ref[...] = ref[z % 2]
        second_ref[...] = ref[(z + 1) % 2]

    return run(body, [shaped((width, length))] * 2, vmem=[value], micros=1, after=after)


def bring_blocks(copies, own_ref, other_ref, wide):
    core, _, z = where_am_i()
    found = []
    for k in range(2):
        slot = (z % 2 + k) % 2
        for ref, user in ((own_ref, core), (other_ref, 1 - core)):
            block = 2 * user + slot
            here = pl.ds(pl.multiple_of(block * QUARTER, QUARTER), QUARTER)
            copies.start(ref.at[k, pl.ds(0, QUARTER)], wide.at[here])
            found.append((ref.at[k], block))
    return found


def prepare_cotangent(own, other, after=()):
    length = own.shape[2]

    def body(own_ref, other_ref, cot_ref, wide, sems):
        copies = Copies(sems)
        bring_blocks(copies, own_ref, other_ref, wide)
        copies.wait()
        cot_ref[...] = wide[...].T

    return run(
        body,
        [shaped((length, D))],
        hbm=[own, other],
        scratch=[pltpu.VMEM((D, length), BF)],
        copies=4,
        micros=3,
        after=after,
    )[0]


def prepare(own, other, corpus_weights):
    length = own.shape[2]

    def body(
        weights_ref, own_ref, other_ref, hidden_ref, norms_ref, nums_ref, wide, extra, sems
    ):
        copies = Copies(sems)
        for ref, block in bring_blocks(copies, own_ref, other_ref, wide):
            copies.start(ref.at[pl.ds(QUARTER, 32)], extra.at[block])
        copies.wait()
        hidden_ref[...] = wide[...].T
        parts = [extra[b].astype(F32) for b in range(4)]
        norms_ref[...] = jnp.concatenate(
            [(e[0:8] + e[8:16] + e[16:24])[:, :QUARTER] for e in parts], axis=1
        )
        row = parts[0][24:25]
        tok = 256.0 * row[:, 0:1] + row[:, 1:2]
        aud = 256.0 * row[:, 2:3] + row[:, 3:4]
        weights = weights_ref[...]
        places = lax.broadcasted_iota(jnp.int32, weights.shape, 1).astype(F32)
        weight = jnp.sum(jnp.where(places == row[:, 4:5], weights, 0.0), axis=1, keepdims=True)
        index = lax.broadcasted_iota(jnp.int32, (8, 128), 0)
        nums_ref[...] = jnp.where(index == 0, tok, jnp.where(index == 1, aud, weight))

    return run(
        body,
        [shaped((length, D)), shaped((8, D), F32), shaped((8, 128), F32)],
        vmem=[corpus_weights.reshape(1, -1)],
        hbm=[own, other],
        scratch=[pltpu.VMEM((D, length), BF), pltpu.VMEM((4, 32, length), BF)],
        copies=8,
        micros=3,
    )


def quarters(value):
    return jnp.concatenate([value[:, p * QUARTER : (p + 1) * QUARTER] for p in range(4)], axis=0)


def attention_shard(self_qkv, self_out, cross_kv, cross_q, cross_out):
    rows = cross_q.shape[0]

    def body(qkv_ref, out_ref, kv_ref, q_ref, cout_ref, shard_ref):
        out = quarters(out_ref[...].astype(F32)).astype(BF)
        cout = quarters(cout_ref[...].astype(F32)).astype(BF)
        shard_ref[...] = jnp.concatenate(
            [qkv_ref[j] for j in range(3)] + [out, kv_ref[...], q_ref[...], cout], axis=1
        )

    return run(
        body,
        [shaped((rows, 2 * D))],
        vmem=[self_qkv.transpose(1, 0, 2), self_out, cross_kv.reshape(rows, -1), cross_q, cross_out],
        micros=2,
    )[0]


def column_slots():
    core, _, z = where_am_i()
    j = z % 2
    home = 1 - jnp.abs(z // 2 - core)
    same = core + (1 - 2 * core) * (1 - home)
    return home == 1, (2 * (1 - j) + same, 2 * j + 1 - same, 2 * (1 - j) + 1 - same, 2 * j + same)


def bring_column(part_refs, own_ref, shards, sems):
    home, slots = column_slots()
    copies = Copies(sems)
    for k in range(3):
        copies.start(part_refs[k], shards.at[slots[k]])

    @pl.when(home)
    def _():
        copy = pltpu.make_async_copy(own_ref, shards.at[slots[3]], sems.at[3])
        copy.start()
        copy.wait()

    @pl.when(jnp.logical_not(home))
    def _():
        copy = pltpu.make_async_copy(part_refs[3], shards.at[slots[3]], sems.at[3])
        copy.start()
        copy.wait()

    copies.wait()


def pack_attention(parts, own, after):
    rows = own.shape[0]
    few = rows // 4

    def body(*refs):
        part_refs, own_ref, (out_ref, shards, sems) = refs[:4], refs[4], refs[5:]
        bring_column(part_refs, own_ref, shards, sems)
        for which in range(2):
            for cs in range(2):
                low, high = shards[cs], shards[2 + cs]

                def both(at):
                    at = at + which * D
                    return [low[:, at : at + QUARTER], high[:, at : at + QUARTER]]

                here = pl.ds(cs * rows, rows)
                out_ref[0, which, here, :] = jnp.concatenate(both(0) + both(QUARTER), axis=1)
                out_ref[1, which, here, 0:HALF] = jnp.concatenate(both(HALF), axis=1)
            at = 3 * QUARTER + which * D
            outs = [shards[i, :, at : at + QUARTER].astype(F32) for i in range(4)]
            stack = []
            for q in range(2):
                for i in range(4):
                    left = outs[i][2 * q * few : (2 * q + 1) * few]
                    right = outs[i][(2 * q + 1) * few : (2 * q + 2) * few]
                    stack.append(jnp.concatenate([left, right], axis=1))
            out_ref[1, which, :, HALF:D] = jnp.concatenate(stack, axis=0).astype(BF)

    return run(
        body,
        [shaped((2, 2, 2 * rows, D))],
        hbm=list(parts) + [own],
        scratch=[pltpu.VMEM((4, rows, 2 * D), BF)],
        copies=4,
        micros=2,
        after=after,
    )[0]


def unit_shard(place, fc_in, fc_out):
    rows = fc_in.shape[0]
    both = fc_in.reshape(rows, place.chips, 2, rows).transpose(2, 0, 1, 3).reshape(2, rows, HALF)
    kept = lax.dynamic_index_in_dim(both, place.core, 0, keepdims=False)
    sent = lax.dynamic_index_in_dim(both, 1 - place.core, 0, keepdims=False)
    came = place.swap_core(sent)
    first = place.core == 0
    left = jnp.concatenate([jnp.where(first, kept, came), jnp.where(first, came, kept)])
    right = jnp.concatenate([fc_out[:, :HALF], fc_out[:, HALF:]])
    return jnp.concatenate([left, right], axis=1)


def stack_units(blocks, after):
    rows = blocks[0].shape[0]

    def body(*refs):
        for k in range(4):
            refs[4][k // 2, k % 2] = refs[k][...]

    return run(body, [shaped((2, 2, rows, D))], vmem=blocks, micros=1.5, after=after)[0]


def gather_units(place, shard):
    whole = lax.all_gather(shard, CHIPS, axis=0)
    rows = shard.shape[0] // 2
    whole = whole.reshape(place.chips, place.mp, 2 * rows, D)
    up = whole[..., :HALF].transpose(0, 2, 1, 3).reshape(D, 2 * D)
    down = whole[..., HALF:].reshape(place.chips, place.mp, 2, rows, HALF)
    return [up, down.transpose(1, 0, 3, 2, 4).reshape(2 * D, D)]


def scatter_units(place, grads, after=()):
    axes = "mp" if place.fast else CHIPS
    total = lax.psum_scatter(grads, axes, scatter_dimension=0, tiled=False)
    rows = total.shape[0] // 2
    if not place.fast:
        kept = lax.dynamic_slice_in_dim(total, place.core * rows, rows, 0)
        sent = lax.dynamic_slice_in_dim(total[:, :HALF], (1 - place.core) * rows, rows, 0)
        came = place.swap_core(sent)
        kept = kept[:, :HALF]
        first = place.core == 0
        both = jnp.stack([jnp.where(first, kept, came), jnp.where(first, came, kept)])
        both = both.reshape(2, rows, place.chips, rows).transpose(1, 2, 0, 3).reshape(rows, D)
        down = jnp.concatenate([total[:rows, HALF:], total[rows:, HALF:]], axis=1)
        return both.astype(F32), down.astype(F32)

    def cut(total_ref, kept_ref, sent_ref, down_ref):
        core, _, _ = where_am_i()
        mine = pl.ds(pl.multiple_of(core * rows, 16), rows)
        theirs = pl.ds(pl.multiple_of((1 - core) * rows, 16), rows)
        kept_ref[...] = total_ref[mine, 0:HALF]
        sent_ref[...] = total_ref[theirs, 0:HALF]
        down_ref[:, 0:HALF] = total_ref[0:rows, HALF:D].astype(F32)
        down_ref[:, HALF:D] = total_ref[rows : 2 * rows, HALF:D].astype(F32)

    kept, sent, down = run(
        cut,
        [shaped((rows, HALF)), shaped((rows, HALF)), shaped((rows, D), F32)],
        vmem=[total],
        micros=1,
        after=after,
    )

    def join(kept_ref, came_ref, up_ref, both):
        core, _, _ = where_am_i()
        both[core] = kept_ref[...]
        both[1 - core] = came_ref[...]
        blocks = []
        for chip in range(place.chips):
            for parity in range(2):
                blocks.append(both[parity, :, chip * rows : (chip + 1) * rows].astype(F32))
        up_ref[...] = jnp.concatenate(blocks, axis=1)

    up = run(
        join,
        [shaped((rows, D), F32)],
        vmem=[kept, place.swap_core(sent)],
        scratch=[pltpu.VMEM((2, rows, HALF), BF)],
        micros=1,
    )[0]
    return up, down


def spread(place, own):
    from_x = place.swap_xy(own, 1)
    from_y = place.swap_xy(own, 2)
    far_one = place.swap_xy(from_y[1], 1)
    far_zero = place.swap_xy(from_x[0], 2)
    return [own, from_x, from_y, far_zero, far_one]


def piece_views(refs, message, which, xy):
    own, from_x, from_y, far_zero, far_one = refs
    return [
        (own.at[which, message], xy),
        (from_x.at[which, message], xy ^ 1),
        (from_y.at[which, message], xy ^ 2),
        ((far_zero, far_one)[which].at[message], xy ^ 3),
    ]


def load_wide(copies, refs, message, which, xy, target, columns=None):
    if len(refs) != 5:
        copies.start(refs[which], target)
        return
    for view, chip in piece_views(refs, message, which, xy):
        rows = view.shape[0]
        if columns is not None:
            view = view.at[:, pl.ds(0, columns)]
        copies.start(view, target.at[pl.ds(pl.multiple_of(chip * rows, 16), rows)])


def load_out(copies, refs, message, xy, target):
    if len(refs) != 5:
        copies.start(refs[2], target)
        return
    for view, chip in piece_views(refs, message, 1, xy):
        rows = view.shape[0] // 4
        for q in range(2):
            for hi in range(2):
                copies.start(
                    view.at[pl.ds((2 * q + hi) * rows, rows), pl.ds(HALF, HALF)],
                    target.at[q, pl.ds(pl.multiple_of(hi * QUARTER + chip * rows, 16), rows)],
                )


def unit_views(refs):
    _, xy, z = where_am_i()
    views = []
    for part in range(2):
        for view, chip in [
            (refs[0].at[part], xy),
            (refs[1].at[part], xy ^ 1),
            (refs[2].at[part], xy ^ 2),
            (refs[3 + part], xy ^ 3),
        ]:
            for i in range(2):
                views.append((view.at[i], chip, z ^ (2 * part + i)))
    return views


def load_up(copies, refs, w_up):
    if len(refs) == 2:
        copies.start(refs[0], w_up)
        return
    for view, chip, z in unit_views(refs):
        rows = view.shape[0]
        copies.start(
            view.at[:, pl.ds(0, HALF)],
            w_up.at[
                pl.ds(pl.multiple_of(rows * chip, 16), rows), pl.ds(pl.multiple_of(z * HALF, HALF), HALF)
            ],
        )


def load_down(copies, refs, w_down):
    if len(refs) == 2:
        copies.start(refs[1], w_down)
        return
    for view, chip, z in unit_views(refs):
        rows = view.shape[0] // 2
        for q in range(2):
            copies.start(
                view.at[pl.ds(q * rows, rows), pl.ds(HALF, HALF)],
                w_down.at[
                    pl.ds(pl.multiple_of(z * HALF + chip * rows, 16), rows), pl.ds(q * HALF, HALF)
                ],
            )


ATTENTION_COPIES = 4 + 4 + 16
UP_COPIES = 16
DOWN_COPIES = 32


def gather_plain(place, shard):
    whole = lax.all_gather(shard, ("mp", "xy", "core"), axis=0)
    whole = whole.reshape((2, 2, place.dp) + shard.shape)
    return lax.dynamic_index_in_dim(whole, place.core, 0, keepdims=False)


def attention_plain(place, shard):
    mine = gather_plain(place, shard)
    rows = shard.shape[0]

    def columns(at, count):
        value = mine[..., at : at + count * QUARTER].reshape(2, D, count, QUARTER)
        return value.transpose(1, 2, 0, 3).reshape(D, count * HALF)

    out = mine[..., 3 * QUARTER :].reshape(2, place.dp, 2, 2, rows // 4, QUARTER)
    out = out.transpose(2, 0, 1, 4, 3, 5).reshape(2, HALF, HALF)
    return [columns(0, 2), columns(HALF, 1), out]


def head_rows(h):
    return pl.ds(pl.multiple_of(h * HEAD_DIM, HEAD_DIM), HEAD_DIM)


def low_parts(value):
    parts = []
    for _ in range(3):
        part = value.astype(BF)
        parts.append(part)
        value = value - part.astype(F32)
    return parts


def widened(count):
    return lambda rows: (
        lax.broadcasted_iota(jnp.int32, (rows, HEAD_DIM), 1) < count
    ).astype(F32).astype(BF)


def below(head, rows):
    blank = jnp.zeros((HEAD_DIM - len(rows), head.shape[1]), F32)
    rest = jnp.concatenate([row.astype(F32) for row in rows] + [blank], axis=0)
    return jnp.concatenate([head, rest.astype(BF)], axis=0)


def project(left, pair_ref):
    return jnp.concatenate([mm(left, pair_ref[0]), mm(left, pair_ref[1])], axis=1)


def project_t(left, pair_ref):
    return mm_t(left[:, :HALF], pair_ref[0]) + mm_t(left[:, HALF:], pair_ref[1])


def self_forward(hidden, norms, nums, weights, after=()):
    length = hidden.shape[0]

    def body(hidden_ref, norms_ref, nums_ref, *refs):
        w_refs, refs = refs[: len(weights)], refs[len(weights) :]
        part_ref, at_ref, qkv_ref, qt_ref, kt_ref, ot_ref, lse_ref = refs[:7]
        w_qk, w_v, w_out, vt, heads, bias, sems = refs[7:]
        _, xy, _ = where_am_i()
        copies = Copies(sems)
        load_wide(copies, w_refs, 0, 0, xy, w_qk)
        load_wide(copies, w_refs, 0, 1, xy, w_v, HALF)
        load_out(copies, w_refs, 0, xy, w_out)
        unit, _ = norm(hidden_ref[...].astype(F32))
        a = (unit * norms_ref[0:1] + norms_ref[4:5]).astype(BF)
        at_ref[...] = a.T
        keys = lax.broadcasted_iota(jnp.int32, (length, length), 0)
        queries = lax.broadcasted_iota(jnp.int32, (length, length), 1)
        allowed = (keys <= queries) & (keys.astype(F32) < nums_ref[0:1, 0:1])
        bias[...] = jnp.where(allowed, 0.0, -1e30)
        copies.wait()
        qk = mm(a, w_qk[...])
        q = (qk[:, :HALF].astype(BF).astype(F32) * HEAD_DIM ** (-0.5)).astype(BF)
        k = qk[:, HALF:].astype(BF)
        v = mm(a, w_v[...]).astype(BF)
        qkv_ref[:, 0:HALF] = q
        qkv_ref[:, HALF : 2 * HALF] = k
        qkv_ref[:, 2 * HALF :] = v
        qt_ref[...] = q.T
        kt_ref[...] = k.T
        vt[...] = v.T
        for h in range(HEADS):
            heads[h] = k[:, h * HEAD_DIM : (h + 1) * HEAD_DIM]

        def head(h, carry):
            s = mm(heads[h], qt_ref[head_rows(h), :]) + bias[...]
            top = jnp.max(s, axis=0, keepdims=True)
            p = jnp.exp(s - top)
            total = jnp.sum(p, axis=0, keepdims=True)
            o = mm(vt[head_rows(h), :], p.astype(BF))
            ot_ref[head_rows(h), :] = (o / total).astype(BF)
            lse_ref[h] = top + jnp.log(total)
            return carry

        lax.fori_loop(0, HEADS, head, 0)
        part_ref[...] = project(ot_ref[...].T, w_out).astype(BF)

    return run(
        body,
        [
            shaped((length, D)),
            shaped((D, length)),
            shaped((length, 3 * HALF)),
            shaped((HALF, length)),
            shaped((HALF, length)),
            shaped((HALF, length)),
            shaped((HEADS, 1, length), F32),
        ],
        vmem=[hidden, norms, nums],
        hbm=weights,
        scratch=[
            pltpu.VMEM((D, D), BF),
            pltpu.VMEM((D, HALF), BF),
            pltpu.VMEM((2, HALF, HALF), BF),
            pltpu.VMEM((HALF, length), BF),
            pltpu.VMEM((HEADS, length, HEAD_DIM), BF),
            pltpu.VMEM((length, length), F32),
        ],
        copies=ATTENTION_COPIES,
        micros=10,
        after=after,
    )


def turn(value, after=()):
    rows, columns = value.shape

    def body(ref, out_ref):
        for at in range(0, rows, CHUNK):
            out_ref[:, at : at + CHUNK] = ref[at : at + CHUNK, :].T

    return run(body, [shaped((columns, rows))], vmem=[value], micros=4, after=after)[0]


def cross_memory(encoded, weights):
    frames = encoded.shape[0]

    def body(enc_ref, *refs):
        w_refs, refs = refs[: len(weights)], refs[len(weights) :]
        kv_ref, kvt_ref, w_kv, sems = refs
        _, xy, _ = where_am_i()
        copies = Copies(sems)
        load_wide(copies, w_refs, 1, 0, xy, w_kv)
        copies.wait()

        def step(i, carry):
            here = pl.ds(pl.multiple_of(i * CHUNK, CHUNK), CHUNK)
            kv = mm(enc_ref[here, :], w_kv[...]).astype(BF)
            kv_ref[here, :] = kv
            kvt_ref[:, here] = kv.T
            return carry

        lax.fori_loop(0, frames // CHUNK, step, 0)

    return run(
        body,
        [shaped((frames, D)), shaped((D, frames))],
        vmem=[encoded],
        hbm=weights,
        scratch=[pltpu.VMEM((D, D), BF)],
        copies=4,
        micros=6,
    )


def residual(hidden_ref, mine_ref, other_ref):
    return hidden_ref[...].astype(F32) + (mine_ref[...].astype(F32) + other_ref[...].astype(F32))


def cross_forward(hidden, mine, other, norms, nums, kv, kvt, weights):
    length = hidden.shape[0]
    frames = kv.shape[0]

    def body(hidden_ref, mine_ref, other_ref, norms_ref, nums_ref, kv_ref, kvt_ref, *refs):
        w_refs, refs = refs[: len(weights)], refs[len(weights) :]
        part_ref, h_ref, ct_ref, q_ref, qt_ref, ot_ref, lse_ref = refs[:7]
        w_q, w_out, heads, values_t, scores, sems = refs[7:]
        _, xy, _ = where_am_i()
        copies = Copies(sems)
        load_wide(copies, w_refs, 1, 1, xy, w_q, HALF)
        load_out(copies, w_refs, 1, xy, w_out)
        h1 = residual(hidden_ref, mine_ref, other_ref)
        h_ref[...] = h1
        unit, _ = norm(h1)
        c = (unit * norms_ref[1:2] + norms_ref[5:6]).astype(BF)
        ct_ref[...] = c.T
        frame = lax.broadcasted_iota(jnp.int32, (frames, HEAD_DIM), 0).astype(F32)
        lane = lax.broadcasted_iota(jnp.int32, (frames, HEAD_DIM), 1)
        mask = jnp.where(frame < nums_ref[1:2, 0:1], 0.0, -1e30)
        beside = jnp.where(lane == 0, mask, 0.0).astype(BF)
        one = lax.broadcasted_iota(jnp.int32, (16, frames), 0)
        one = jnp.where(one == 0, 1.0, 0.0).astype(BF)
        for h in range(HEADS):
            keys = kv_ref[:, h * HEAD_DIM : (h + 1) * HEAD_DIM]
            heads[h] = jnp.concatenate([keys, beside], axis=1)
            values = kvt_ref[HALF + h * HEAD_DIM : HALF + (h + 1) * HEAD_DIM, :]
            values_t[h] = jnp.concatenate([values, one], axis=0)
        copies.wait()
        q = mm(c, w_q[...]).astype(BF)
        q = (q.astype(F32) * HEAD_DIM ** (-0.5)).astype(BF)
        q_ref[...] = q
        qt_ref[...] = q.T
        ones = jnp.ones((1, length), F32)

        def head(h, carry):
            qt = below(qt_ref[head_rows(h), :], [ones])
            top = None
            for at in range(0, frames, CHUNK):
                s = mm(heads[h, at : at + CHUNK], qt)
                scores[at : at + CHUNK] = s
                high = jnp.max(s, axis=0, keepdims=True)
                top = high if top is None else jnp.maximum(top, high)
            o = None
            for at in range(0, frames, CHUNK):
                p = jnp.exp(scores[at : at + CHUNK] - top).astype(BF)
                more = mm(values_t[h, :, at : at + CHUNK], p)
                o = more if o is None else o + more
            total = o[HEAD_DIM : HEAD_DIM + 1]
            ot_ref[head_rows(h), :] = (o[:HEAD_DIM] / total).astype(BF)
            lse_ref[h] = top + jnp.log(total)
            return carry

        lax.fori_loop(0, HEADS, head, 0)
        part_ref[...] = project(ot_ref[...].T, w_out).astype(BF)

    return run(
        body,
        [
            shaped((length, D)),
            shaped((length, D), F32),
            shaped((D, length)),
            shaped((length, HALF)),
            shaped((HALF, length)),
            shaped((HALF, length)),
            shaped((HEADS, 1, length), F32),
        ],
        vmem=[hidden, mine, other, norms, nums, kv, kvt],
        hbm=weights,
        scratch=[
            pltpu.VMEM((D, HALF), BF),
            pltpu.VMEM((2, HALF, HALF), BF),
            pltpu.VMEM((HEADS, frames, 2 * HEAD_DIM), BF),
            pltpu.VMEM((HEADS, HEAD_DIM + 16, frames), BF),
            pltpu.VMEM((frames, length), F32),
        ],
        copies=4 + 16,
        micros=10,
    )


def units_forward(hidden, mine, other, norms, weights):
    length = hidden.shape[0]

    def body(hidden_ref, mine_ref, other_ref, norms_ref, *refs):
        w_refs, refs = refs[: len(weights)], refs[len(weights) :]
        part_ref, h_ref, mt_ref, slope_ref, it_ref = refs[:5]
        w_up, w_down, inner, late_sems, sems = refs[5:]
        _, xy, _ = where_am_i()
        copies = Copies(sems)
        load_up(copies, w_refs, w_up)
        late = Copies(late_sems)
        load_down(late, w_refs, w_down)
        h2 = residual(hidden_ref, mine_ref, other_ref)
        h_ref[...] = h2
        unit, _ = norm(h2)
        m = (unit * norms_ref[2:3] + norms_ref[6:7]).astype(BF)
        mt_ref[...] = m.T
        copies.wait()
        for at in range(0, 2 * D, CHUNK):
            here = slice(at, at + CHUNK)
            z = mm(m, w_up[:, here])
            share = 0.5 * (1.0 + lax.erf(z * 0.7071067811865476))
            slope = share + z * (0.3989422804014327 * jnp.exp(-0.5 * z * z))
            value = (z * share).astype(BF)
            inner[:, here] = value
            it_ref[here, :] = value.T
            slope_ref[:, here] = slope.astype(BF)
        late.wait()
        for at in range(0, D, CHUNK):
            part_ref[:, at : at + CHUNK] = mm(inner[...], w_down[:, at : at + CHUNK]).astype(BF)

    return run(
        body,
        [
            shaped((length, D)),
            shaped((length, D), F32),
            shaped((D, length)),
            shaped((length, 2 * D)),
            shaped((2 * D, length)),
        ],
        vmem=[hidden, mine, other, norms],
        hbm=weights,
        scratch=[
            pltpu.VMEM((D, 2 * D), BF),
            pltpu.VMEM((2 * D, D), BF),
            pltpu.VMEM((length, 2 * D), BF),
            pltpu.SemaphoreType.DMA((DOWN_COPIES,)),
        ],
        copies=UP_COPIES,
        micros=9,
    )


def store_blocks(value, blocks, first_ref, second_ref):
    core, _, z = where_am_i()
    for b in range(4):
        blocks[b] = value[:, b * QUARTER : (b + 1) * QUARTER]
    first_ref[...] = blocks[2 * core + z % 2].T
    second_ref[...] = blocks[2 * core + (z + 1) % 2].T


def units_backward(hidden, mine, other, norms, nums, cot, slope, weights):
    length = hidden.shape[0]

    def body(hidden_ref, mine_ref, other_ref, norms_ref, nums_ref, cot_ref, slope_ref, *refs):
        w_refs, refs = refs[: len(weights)], refs[len(weights) :]
        part_ref, d_ref, e_ref, dz_ref, terms_ref, first_ref, second_ref = refs[:7]
        w_up, w_down, blocks, late_sems, sems = refs[7:]
        _, xy, _ = where_am_i()
        copies = Copies(sems)
        load_down(copies, w_refs, w_down)
        late = Copies(late_sems)
        load_up(late, w_refs, w_up)
        unit, inverse = norm(residual(hidden_ref, mine_ref, other_ref))
        final = (unit * norms_ref[3:4] + norms_ref[7:8]).astype(BF)
        store_blocks(final, blocks, first_ref, second_ref)
        live = lax.broadcasted_iota(jnp.int32, (length, 1), 0).astype(F32) < nums_ref[0:1, 0:1]
        grad = cot_ref[...].astype(F32) * jnp.where(live, nums_ref[2:3, 0:1], 0.0)
        d3, terms = norm_back(grad, unit, inverse, norms_ref[3:4])
        d_ref[...] = d3
        terms_ref[...] = terms
        e = d3.astype(BF)
        e_ref[...] = e
        copies.wait()
        for at in range(0, 2 * D, CHUNK):
            here = slice(at, at + CHUNK)
            d_inner = mm_t(e, w_down[here, :])
            dz_ref[:, here] = (slope_ref[:, here].astype(F32) * d_inner).astype(BF)
        late.wait()
        for at in range(0, D, CHUNK):
            out = mm_t(dz_ref[...], w_up[at : at + CHUNK, :])
            part_ref[:, at : at + CHUNK] = out.astype(BF)

    return run(
        body,
        [
            shaped((length, D)),
            shaped((length, D), F32),
            shaped((length, D)),
            shaped((length, 2 * D)),
            shaped((2, D), F32),
            shaped((QUARTER, length)),
            shaped((QUARTER, length)),
        ],
        vmem=[hidden, mine, other, norms, nums, cot, slope],
        hbm=weights,
        scratch=[
            pltpu.VMEM((D, 2 * D), BF),
            pltpu.VMEM((2 * D, D), BF),
            pltpu.VMEM((4, length, QUARTER), BF),
            pltpu.SemaphoreType.DMA((UP_COPIES,)),
        ],
        copies=DOWN_COPIES,
        micros=10,
    )


def step_back(d_ref, hidden_ref, mine_ref, other_ref, gain):
    unit, inverse = norm(hidden_ref[...].astype(F32))
    grad = mine_ref[...].astype(F32) + other_ref[...].astype(F32)
    part, terms = norm_back(grad, unit, inverse, gain)
    return d_ref[...] + part, terms


def cross_backward(
    d, hidden, mine, other, norms, nums, kv, kvt, q, qt, ot, lse, weights, after=()
):
    length = hidden.shape[0]
    frames = kv.shape[0]

    def body(
        d_ref, hidden_ref, mine_ref, other_ref, norms_ref, nums_ref, kv_ref, kvt_ref, q_ref,
        qt_ref, ot_ref, lse_ref, *refs
    ):
        w_refs, refs = refs[: len(weights)], refs[len(weights) :]
        part_ref, d_out_ref, e_ref, dq_ref, dkv_ref, terms_ref = refs[:6]
        w_q, w_out, keys, values, queries, grads, dot_t, dk_h, dv_h, dqt, sems = refs[6:]
        _, xy, _ = where_am_i()
        copies = Copies(sems)
        load_wide(copies, w_refs, 1, 1, xy, w_q, HALF)
        load_out(copies, w_refs, 1, xy, w_out)
        d2, terms = step_back(d_ref, hidden_ref, mine_ref, other_ref, norms_ref[2:3])
        d_out_ref[...] = d2
        terms_ref[...] = terms
        e = d2.astype(BF)
        e_ref[...] = e
        frame = lax.broadcasted_iota(jnp.int32, (frames, HEAD_DIM), 0).astype(F32)
        lane = lax.broadcasted_iota(jnp.int32, (frames, HEAD_DIM), 1)
        mask = jnp.where(frame < nums_ref[1:2, 0:1], 0.0, -1e30)
        beside = jnp.where(lane == 0, mask, jnp.where(lane < 4, 1.0, 0.0)).astype(BF)
        three = widened(3)(frames)
        for h in range(HEADS):
            lanes = slice(h * HEAD_DIM, (h + 1) * HEAD_DIM)
            keys[h] = jnp.concatenate([kv_ref[:, lanes], beside], axis=1)
            value = kv_ref[:, HALF + h * HEAD_DIM : HALF + (h + 1) * HEAD_DIM]
            values[h] = jnp.concatenate([value, three], axis=1)
            queries[h] = q_ref[:, lanes]
        copies.wait()
        d_mixed = project_t(e, w_out).astype(BF)
        dot_t[...] = d_mixed.T
        for h in range(HEADS):
            grads[h] = d_mixed[:, h * HEAD_DIM : (h + 1) * HEAD_DIM]
        ones = jnp.ones((1, length), F32)

        def head(h, carry):
            rows = head_rows(h)
            do_t = dot_t[rows, :]
            q_n, do_n = queries[h], grads[h]
            delta = jnp.sum(do_t.astype(F32) * ot_ref[rows, :].astype(F32), axis=0, keepdims=True)
            q_t = below(qt_ref[rows, :], [ones] + low_parts(-lse_ref[h]))
            do_t = below(do_t, low_parts(-delta))
            total = None
            for at in range(0, frames, CHUNK):
                here = slice(at, at + CHUNK)
                p = jnp.exp(mm(keys[h, here], q_t))
                ds = (p * mm(values[h, here], do_t)).astype(BF)
                dv_h[h, here] = mm(p.astype(BF), do_n).astype(BF)
                dk_h[h, here] = mm(ds, q_n).astype(BF)
                more = mm(kvt_ref[rows, here], ds)
                total = more if total is None else total + more
            dqt[rows, :] = (total * HEAD_DIM ** (-0.5)).astype(BF)
            return carry

        lax.fori_loop(0, HEADS, head, 0)
        dq = dqt[...].T
        dq_ref[...] = dq
        part_ref[...] = mm_t(dq, w_q[...]).astype(BF)
        for h in range(HEADS):
            lanes = slice(h * HEAD_DIM, (h + 1) * HEAD_DIM)
            dkv_ref[:, lanes] = dk_h[h]
            dkv_ref[:, HALF + h * HEAD_DIM : HALF + (h + 1) * HEAD_DIM] = dv_h[h]

    return run(
        body,
        [
            shaped((length, D)),
            shaped((length, D), F32),
            shaped((length, D)),
            shaped((length, HALF)),
            shaped((frames, D)),
            shaped((2, D), F32),
        ],
        vmem=[d, hidden, mine, other, norms, nums, kv, kvt, q, qt, ot, lse],
        hbm=weights,
        scratch=[
            pltpu.VMEM((D, HALF), BF),
            pltpu.VMEM((2, HALF, HALF), BF),
            pltpu.VMEM((HEADS, frames, 2 * HEAD_DIM), BF),
            pltpu.VMEM((HEADS, frames, 2 * HEAD_DIM), BF),
            pltpu.VMEM((HEADS, length, HEAD_DIM), BF),
            pltpu.VMEM((HEADS, length, HEAD_DIM), BF),
            pltpu.VMEM((HALF, length), BF),
            pltpu.VMEM((HEADS, frames, HEAD_DIM), BF),
            pltpu.VMEM((HEADS, frames, HEAD_DIM), BF),
            pltpu.VMEM((HALF, length), BF),
        ],
        copies=4 + 16,
        micros=22,
        after=after,
    )


def self_backward(d, hidden, mine, other, norms, nums, qkv, qt, kt, ot, lse, weights, after=()):
    length = hidden.shape[0]

    def body(
        d_ref, hidden_ref, mine_ref, other_ref, norms_ref, nums_ref, qkv_ref, qt_ref, kt_ref,
        ot_ref, lse_ref, *refs
    ):
        w_refs, refs = refs[: len(weights)], refs[len(weights) :]
        part_ref, d_out_ref, e_ref, dqk_ref, dv_ref, terms_ref = refs[:6]
        w_qk, w_v, w_out, queries_h, keys, values, grads, dot_t, dk_h, dv_h, dqt, bias, sems = refs[6:]
        _, xy, _ = where_am_i()
        copies = Copies(sems)
        load_out(copies, w_refs, 0, xy, w_out)
        load_wide(copies, w_refs, 0, 0, xy, w_qk)
        load_wide(copies, w_refs, 0, 1, xy, w_v, HALF)
        d1, terms = step_back(d_ref, hidden_ref, mine_ref, other_ref, norms_ref[1:2])
        d_out_ref[...] = d1
        terms_ref[...] = terms
        e = d1.astype(BF)
        e_ref[...] = e
        places = lax.broadcasted_iota(jnp.int32, (length, length), 0)
        queries = lax.broadcasted_iota(jnp.int32, (length, length), 1)
        allowed = (places <= queries) & (places.astype(F32) < nums_ref[0:1, 0:1])
        bias[...] = jnp.where(allowed, 0.0, -1e30)
        three = widened(3)(length)
        for h in range(HEADS):
            at = h * HEAD_DIM
            queries_h[h] = qkv_ref[:, at : at + HEAD_DIM]
            key = qkv_ref[:, HALF + at : HALF + at + HEAD_DIM]
            keys[h] = jnp.concatenate([key, three], axis=1)
            value = qkv_ref[:, 2 * HALF + at : 2 * HALF + at + HEAD_DIM]
            values[h] = jnp.concatenate([value, three], axis=1)
        copies.wait()
        d_mixed = project_t(e, w_out).astype(BF)
        dot_t[...] = d_mixed.T
        for h in range(HEADS):
            grads[h] = d_mixed[:, h * HEAD_DIM : (h + 1) * HEAD_DIM]

        def head(h, carry):
            rows = head_rows(h)
            do_t, do_n = dot_t[rows, :], grads[h]
            delta = jnp.sum(do_t.astype(F32) * ot_ref[rows, :].astype(F32), axis=0, keepdims=True)
            q_t = below(qt_ref[rows, :], low_parts(-lse_ref[h]))
            do_t = below(do_t, low_parts(-delta))
            p = jnp.exp(mm(keys[h], q_t) + bias[...])
            ds = (p * mm(values[h], do_t)).astype(BF)
            dv_h[h] = mm(p.astype(BF), do_n).astype(BF)
            dk_h[h] = mm(ds, queries_h[h]).astype(BF)
            dqt[rows, :] = (mm(kt_ref[rows, :], ds) * HEAD_DIM ** (-0.5)).astype(BF)
            return carry

        lax.fori_loop(0, HEADS, head, 0)
        dqk_ref[:, 0:HALF] = dqt[...].T
        for h in range(HEADS):
            lanes = slice(HALF + h * HEAD_DIM, HALF + (h + 1) * HEAD_DIM)
            dqk_ref[:, lanes] = dk_h[h]
            dv_ref[:, h * HEAD_DIM : (h + 1) * HEAD_DIM] = dv_h[h]
        out = mm_t(dqk_ref[...], w_qk[...]) + mm_t(dv_ref[...], w_v[...])
        part_ref[...] = out.astype(BF)

    return run(
        body,
        [
            shaped((length, D)),
            shaped((length, D), F32),
            shaped((length, D)),
            shaped((length, D)),
            shaped((length, HALF)),
            shaped((2, D), F32),
        ],
        vmem=[d, hidden, mine, other, norms, nums, qkv, qt, kt, ot, lse],
        hbm=weights,
        scratch=[
            pltpu.VMEM((D, D), BF),
            pltpu.VMEM((D, HALF), BF),
            pltpu.VMEM((2, HALF, HALF), BF),
            pltpu.VMEM((HEADS, length, HEAD_DIM), BF),
            pltpu.VMEM((HEADS, length, 2 * HEAD_DIM), BF),
            pltpu.VMEM((HEADS, length, 2 * HEAD_DIM), BF),
            pltpu.VMEM((HEADS, length, HEAD_DIM), BF),
            pltpu.VMEM((HALF, length), BF),
            pltpu.VMEM((HEADS, length, HEAD_DIM), BF),
            pltpu.VMEM((HEADS, length, HEAD_DIM), BF),
            pltpu.VMEM((HALF, length), BF),
            pltpu.VMEM((length, length), F32),
        ],
        copies=ATTENTION_COPIES,
        micros=12,
        staged=True,
        after=after,
    )


def finish_hidden(d, hidden, mine, other, norms, terms1, terms2, terms3, after=()):
    length = hidden.shape[0]

    def body(
        d_ref, hidden_ref, mine_ref, other_ref, norms_ref, one, two, three, terms_ref, first_ref,
        second_ref, blocks
    ):
        d0, terms = step_back(d_ref, hidden_ref, mine_ref, other_ref, norms_ref[0:1])
        store_blocks(d0.astype(BF), blocks, first_ref, second_ref)
        for j in range(2):
            here = slice(j, j + 1)
            terms_ref[4 * j : 4 * j + 4] = jnp.concatenate(
                [terms[here], one[here], two[here], three[here]], axis=0
            )

    return run(
        body,
        [shaped((8, D), F32), shaped((QUARTER, length)), shaped((QUARTER, length))],
        vmem=[d, hidden, mine, other, norms, terms1, terms2, terms3],
        scratch=[pltpu.VMEM((4, length, QUARTER), BF)],
        micros=4,
        after=after,
    )


def finish_encoder(keep, other, frames, after=()):
    def body(keep_ref, other_ref, first_ref, second_ref):
        _, _, z = where_am_i()
        for ref, k in ((first_ref, 0), (second_ref, 1)):
            here = pl.ds(pl.multiple_of(((z + k) % 2) * QUARTER, QUARTER), QUARTER)
            total = keep_ref[here, :].astype(F32) + other_ref[here, :].astype(F32)
            ref[...] = total.astype(BF)[:, :frames]

    return run(
        body,
        [shaped((QUARTER, frames)), shaped((QUARTER, frames))],
        vmem=[keep, other],
        micros=2,
        after=after,
    )


def block_plan(place):
    if not place.fast:
        return 1, (((1, 0, 0),), ((1, 0, 0),))
    first = ((1, 0, 0), (0, 0, 1), (1, 1, 2), (0, 1, 3))
    second = ((1, 0, 0), (1, 1, 1), (0, 0, 2), (0, 1, 3))
    return 4, (first, second)


def grad_outputs(place, shape):
    if place.fast:
        return [shaped((2,) + shape)] * 4
    return [shaped((1,) + shape)] * 4


def units_grads(place, mt, dz, it, e):
    chips = place.chips
    rows = D // (2 * chips)
    _, plan = block_plan(place)

    def body(mt_ref, dz_ref, it_ref, e_ref, *outs):
        _, xy, _ = where_am_i()
        for output, slot, offset in plan[1]:
            chip = xy ^ offset
            for z in range(4):
                here = pl.ds(pl.multiple_of(z * HALF + chip * rows, 16), rows)
                outs[2 + output][slot, z] = mm(it_ref[here, :], e_ref[...]).astype(BF)
        for output, slot, offset in plan[0]:
            here = pl.ds(pl.multiple_of((xy ^ offset) * 2 * rows, 16), 2 * rows)
            left = mm(mt_ref[here, :], dz_ref[...]).astype(BF)
            for z in range(4):
                outs[output][slot, z] = left[:, z * HALF : (z + 1) * HALF]

    def plain(mt_ref, dz_ref, it_ref, e_ref, left_ref, right_ref):
        left_ref[...] = mm(mt_ref[...], dz_ref[...]).astype(BF)
        right_ref[...] = mm(it_ref[...], e_ref[...]).astype(BF)

    if place.fast:
        first, second = shaped((2, 4, 2 * rows, HALF)), shaped((2, 4, rows, D))
        return run(
            body, [first, first, second, second], vmem=[mt, dz, it, e], micros=6
        )
    left, right = run(
        plain, [shaped((D, 2 * D)), shaped((2 * D, D))], vmem=[mt, dz, it, e], micros=7
    )
    left = left.reshape(chips, 2 * rows, 4, HALF).transpose(0, 2, 1, 3)
    right = right.reshape(4, chips, rows, 2, HALF).transpose(1, 0, 3, 2, 4)
    whole = jnp.concatenate([left, right.reshape(chips, 4, 2 * rows, HALF)], axis=-1)
    return whole.reshape(4 * chips, 2 * rows, D)


def units_sum(grads, came, onward, after):
    rows = grads[3].shape[2]

    def body(*refs):
        ins, (out_ref, left, right, sems) = refs[:6], refs[6:]
        copies = Copies(sems)
        for i, ref in enumerate(ins):
            target = (left if i < 3 else right).at[i % 3]
            copies.start(ref if i % 3 == 2 else ref.at[0], target)
        copies.wait()
        for z in range(4):
            out_ref[z, :, 0:HALF] = add_up(*[left[i, z] for i in range(3)]).astype(BF)
            down = add_up(*[right[i, z] for i in range(3)]).astype(BF)
            out_ref[z, 0:rows, HALF:D] = down[:, :HALF]
            out_ref[z, rows : 2 * rows, HALF:D] = down[:, HALF:]

    return run(
        body,
        [shaped((4, 2 * rows, D))],
        hbm=[grads[1], came[0], onward[0], grads[3], came[1], onward[1]],
        scratch=[pltpu.VMEM((3, 4, 2 * rows, HALF), BF), pltpu.VMEM((3, 4, rows, D), BF)],
        copies=6,
        micros=3,
        after=after,
    )[0]


def attention_grads(place, wide_left, wide_right, left, right, ot, e, after=()):
    count, plan = block_plan(place)
    rows = D // count
    few = rows // 4

    def body(wide_left_ref, wide_right_ref, left_ref, right_ref, ot_ref, e_ref, *outs):
        _, xy, _ = where_am_i()
        for output, slot, offset in plan[0]:
            chip = xy ^ offset if count > 1 else 0
            here = pl.ds(pl.multiple_of(chip * rows, 16), rows)
            outs[output][slot] = mm(wide_left_ref[here, :], wide_right_ref[...]).astype(BF)
        for output, slot, offset in plan[1]:
            chip = xy ^ offset if count > 1 else 0
            here = pl.ds(pl.multiple_of(chip * rows, 16), rows)
            target = outs[2 + output]
            target[slot, :, 0:HALF] = mm(left_ref[here, :], right_ref[...]).astype(BF)
            for hi in range(2):
                here = pl.ds(pl.multiple_of(hi * QUARTER + chip * few, 16), few)
                both = mm(ot_ref[here, :], e_ref[...]).astype(BF)
                for q in range(2):
                    at = (2 * q + hi) * few
                    target[slot, at : at + few, HALF:D] = both[:, q * HALF : (q + 1) * HALF]

    return run(
        body,
        grad_outputs(place, (rows, D)),
        vmem=[wide_left, wide_right, left, right, ot, e],
        micros=6,
        after=after,
    )


def encoder_grad(dkv, weights, after=()):
    padded = dkv.shape[0]

    def body(dkv_ref, *refs):
        w_refs, (keep_ref, send_ref, w_kv, sems) = refs[: len(weights)], refs[len(weights) :]
        core, xy, _ = where_am_i()
        copies = Copies(sems)
        load_wide(copies, w_refs, 1, 0, xy, w_kv)
        copies.wait()
        mine = pl.ds(pl.multiple_of(core * HALF, HALF), HALF)
        theirs = pl.ds(pl.multiple_of((1 - core) * HALF, HALF), HALF)
        for ref, rows in ((send_ref, theirs), (keep_ref, mine)):
            for at in range(0, padded, CHUNK):
                value = mm_t(w_kv[rows, :], dkv_ref[at : at + CHUNK, :])
                ref[:, at : at + CHUNK] = value.astype(BF)

    return run(
        body,
        [shaped((HALF, padded)), shaped((HALF, padded))],
        vmem=[dkv],
        hbm=weights,
        scratch=[pltpu.VMEM((D, D), BF)],
        copies=4,
        micros=3.5,
        after=after,
    )


def leave_plane(place, grads):
    return [place.swap_xy(grads[0], 1), place.swap_xy(grads[2], 2)]


def pass_on(grads, came, after):
    shapes = [grads[1].shape[1:], grads[3].shape[1:]]

    def body(stay0, came0, stay1, came1, out0, out1, held0, held1, sems):
        copies = Copies(sems)
        for i, ref in enumerate((stay0, came0, stay1, came1)):
            copies.start(ref.at[1], (held0 if i < 2 else held1).at[i % 2])
        copies.wait()
        out0[...] = add_up(held0[0], held0[1]).astype(BF)
        out1[...] = add_up(held1[0], held1[1]).astype(BF)

    return run(
        body,
        [shaped(shape) for shape in shapes],
        hbm=[grads[1], came[0], grads[3], came[1]],
        scratch=[pltpu.VMEM((2,) + shape, BF) for shape in shapes],
        copies=4,
        micros=1,
        after=after,
    )


def cross_plane(place, onward):
    return [place.swap_xy(onward[0], 2), place.swap_xy(onward[1], 1)]


def column_blocks(grads, came, onward, swapped, norm_terms=(), after=()):
    shape = onward[0].shape
    rows = shape[-2] // 2
    width = D
    few = rows // 4
    extra = 16 if norm_terms else 0

    def body(*refs):
        terms_refs, refs = refs[: len(norm_terms)], refs[len(norm_terms) :]
        ins, outs, (held, shards, sems) = refs[:6], refs[6:-3], refs[-3:]
        home, slots = column_slots()
        copies = Copies(sems)
        for i, ref in enumerate(ins):
            copies.start(ref if i % 3 == 2 else ref.at[0], held.at[i])
        copies.wait()
        sums = [add_up(held[3 * part], held[3 * part + 1], held[3 * part + 2]) for part in range(2)]
        for hi in range(2):
            for cs in range(2):
                here = slice(cs * rows, (cs + 1) * rows)
                lanes = slice(hi * QUARTER, (hi + 1) * QUARTER)
                lanes_two = slice(HALF + hi * QUARTER, HALF + (hi + 1) * QUARTER)
                outs_rows = []
                for p in range(4):
                    at = (2 * (p // 2) + hi) * 2 * few + cs * few
                    side = HALF + (p % 2) * QUARTER
                    outs_rows.append(sums[1][at : at + few, side : side + QUARTER])
                value = jnp.concatenate(
                    [
                        sums[0][here, lanes],
                        sums[0][here, lanes_two],
                        sums[1][here, lanes],
                        jnp.concatenate(outs_rows, axis=0),
                    ],
                    axis=1,
                )
                shards[2 * hi + cs, :rows] = value.astype(BF)
        if norm_terms:
            core, xy, _ = where_am_i()
            terms = add_up(*[ref[...] for ref in terms_refs])
            terms = jnp.concatenate([terms, jnp.zeros_like(terms)], axis=0).astype(BF)
            feature = lax.broadcasted_iota(jnp.int32, (D, D), 0)
            lane = lax.broadcasted_iota(jnp.int32, (D, D), 1)
            for hi in range(2):
                for cs in range(2):
                    offset = (2 * core + hi) * QUARTER + (2 * xy + cs) * few
                    pick = jnp.where((feature == lane + offset) & (lane < few), 1.0, 0.0)
                    shards[2 * hi + cs, rows:] = mm(terms, pick.astype(BF)).astype(BF)
        if swapped:
            core, _, _ = where_am_i()
            for hi in range(2):
                outs[0][hi] = shards[2 * hi + core]
                outs[1][hi] = shards[2 * hi + 1 - core]
        else:
            for k in range(4):
                outs[k][...] = shards[slots[k]]

    ins = [grads[1], came[0], onward[0], grads[3], came[1], onward[1]]
    return run(
        body,
        [shaped((2, rows, width))] * 2 if swapped else [shaped((rows + extra, width))] * 4,
        vmem=list(norm_terms),
        hbm=ins,
        after=after,
        scratch=[pltpu.VMEM((6,) + shape, BF), pltpu.VMEM((4, rows + extra, width), BF)],
        copies=6,
        micros=2,
    )


def scatter_column(place, kept, came):
    first = place.core == 0
    both = jnp.concatenate([jnp.where(first, kept, came), jnp.where(first, came, kept)])
    return lax.psum_scatter(both, "mp", scatter_dimension=0, tiled=False)


def sum_plain(place, grads, attention):
    wide, narrow = grads[1][0], grads[3][0]
    rows = D // place.dp
    if attention:
        value = jnp.stack([wide[:, :HALF], wide[:, HALF:], narrow[:, :HALF]], axis=1)
        value = value.reshape(place.dp, rows, 3, 2, QUARTER).transpose(3, 0, 1, 2, 4)
        value = value.reshape(2, place.dp, rows, 3 * QUARTER)
        outs = narrow[:, HALF:].reshape(2, 2, place.dp, rows // 4, 2, QUARTER)
        outs = outs.transpose(1, 2, 0, 4, 3, 5).reshape(2, place.dp, rows, QUARTER)
        value = jnp.concatenate([value, outs], axis=-1)
    else:
        value = jnp.concatenate(
            [wide.reshape(2, place.dp, rows, D), narrow.reshape(2, place.dp, rows, D)], axis=-1
        )
    whole = jnp.zeros((2,) + value.shape, F32)
    whole = lax.dynamic_update_index_in_dim(whole, value.astype(F32), place.core, 0)
    whole = whole.reshape((4 * place.dp,) + value.shape[2:])
    return lax.psum_scatter(whole, ("mp", "xy", "core"), scatter_dimension=0, tiled=False)


def attention_outputs(sums, rows, few):
    value = sums[:rows]
    last = value[:, 3 * QUARTER :]
    out = jnp.concatenate([last[p * few : (p + 1) * few] for p in range(4)], axis=1)
    return [value[:, j * QUARTER : (j + 1) * QUARTER] for j in range(3)], out


def finish_self(got, own, few_lanes):
    rows = own.shape[0] - 16
    few = rows // 4

    def body(a, b, c, d, own_ref, qkv_ref, out_ref, gain_ref, bias_ref):
        home, _ = column_slots()
        last = jnp.where(home, own_ref[...].astype(F32), d[...].astype(F32))
        sums = add_up(a[...], b[...], c[...], last)
        blocks, out = attention_outputs(sums, rows, few)
        for j in range(3):
            qkv_ref[j] = blocks[j]
        out_ref[...] = out
        gain_ref[...] = sums[rows : rows + 4, :few_lanes]
        bias_ref[...] = sums[rows + 4 : rows + 8, :few_lanes]

    return run(
        body,
        [
            shaped((3, rows, QUARTER), F32),
            shaped((few, D), F32),
            shaped((4, few_lanes), F32),
            shaped((4, few_lanes), F32),
        ],
        vmem=list(got) + [own],
        micros=1.5,
    )


def finish_cross(total):
    rows = total.shape[0]
    few = rows // 4

    def body(ref, kv_ref, q_ref, out_ref):
        blocks, out = attention_outputs(ref[...].astype(F32), rows, few)
        kv_ref[...] = jnp.concatenate(blocks[:2], axis=1)
        q_ref[...] = blocks[2]
        out_ref[...] = out

    return run(
        body,
        [shaped((rows, HALF), F32), shaped((rows, QUARTER), F32), shaped((few, D), F32)],
        vmem=[total],
        micros=1.5,
    )


def from_quarters(value):
    few = value.shape[0] // 4
    return value.reshape(4, few, QUARTER).transpose(1, 0, 2).reshape(few, D)


def three_parts(value):
    terms = []
    for _ in range(3):
        term = lax.reduce_precision(value, 8, 7)
        terms.append(term.astype(BF))
        value = value - term
    return jnp.concatenate(terms)


def per_device(
    dp,
    mp,
    hidden_in,
    encoder_states,
    cotangent,
    self_qkv,
    self_out,
    cross_q,
    cross_kv,
    cross_out,
    fc_in,
    fc_out,
    ln_gain,
    ln_bias,
    token_lengths,
    audio_lengths,
    corpus_ids,
    corpus_weights,
):
    place = Place(dp, mp)
    length = hidden_in.shape[2]
    frames = encoder_states.shape[2]
    padded = -(-frames // CHUNK) * CHUNK
    rows = self_qkv.shape[0]

    encoded = lax.dynamic_index_in_dim(encoder_states[:, 0], place.micro, 0, keepdims=False)
    first = ()
    if place.fast:
        shard = attention_shard(self_qkv, self_out, cross_kv, cross_q, cross_out)
        packed = pack_attention(place.column_out(shard), shard, (encoded,))
        w_self = w_cross = spread(place, packed)
        first = (shard,)
        fc_in, packed = lax.optimization_barrier((fc_in, packed))
    else:
        quarter = lambda w: w.reshape(-1, 4, QUARTER).transpose(1, 0, 2).reshape(-1, QUARTER)
        flat = lambda w: w.reshape(rows, -1)
        w_self = attention_plain(
            place, jnp.concatenate([flat(self_qkv), quarter(self_out)], axis=1)
        )
        w_cross = attention_plain(
            place, jnp.concatenate([flat(cross_kv), cross_q, quarter(cross_out)], axis=1)
        )


    unit = unit_shard(place, fc_in, fc_out)
    if not place.fast:
        w_units = gather_units(place, unit)

    turned = lambda value: value[:, 0].transpose(0, 2, 1)
    numbers = jnp.concatenate([token_lengths.T, audio_lengths.T, corpus_ids.T])
    blocks = input_blocks(
        turned(hidden_in),
        three_parts(jnp.concatenate([ln_gain, ln_bias])),
        numbers,
        first,
    )
    got = place.rows_in(blocks)
    if place.fast:
        unit, got = lax.optimization_barrier((unit, got))
        stacked = stack_units(
            [unit] + [place.swap_z(unit, k) for k in (1, 2, 3)], tuple(w_self[3:5])
        )
        w_units = spread(place, stacked)
    hidden, norms, nums = prepare(got, place.swap_core(got), corpus_weights)

    other = place.move(encoded, lambda xy, core, z: (xy, 1 - core, z) if core == z // 2 else None)
    encoded = jnp.where(place.home == place.core, encoded, other)
    encoded = jnp.pad(encoded, ((0, padded - frames), (0, 0)))

    et = turn(encoded)
    part1, at, qkv, qt, kt, ot1, lse1 = self_forward(
        hidden, norms, nums, w_self, (et,) + ((stacked,) if place.fast else ())
    )
    other1 = place.swap_core(part1)
    got = place.rows_in(turned_blocks(turned(cotangent), (at,)))
    kv, kvt = cross_memory(encoded, w_cross)
    part2, h1, ct, q2, qt2, ot2, lse2 = cross_forward(
        hidden, part1, other1, norms, nums, kv, kvt, w_cross
    )
    other2 = place.swap_core(part2)
    cot = prepare_cotangent(got, place.swap_core(got), (part2,))
    part3, h2, mt, slope, it = units_forward(h1, part2, other2, norms, w_units)
    other3 = place.swap_core(part3)
    part, d3, e3, dz, terms3, out_a, out_b = units_backward(
        h2, part3, other3, norms, nums, cot, slope, w_units
    )
    other = place.swap_core(part)
    g_units = units_grads(place, mt, dz, it, e3)
    came_units = leave_plane(place, g_units) if place.fast else None
    layer_got = place.rows_sent((out_a, out_b))
    layer_out = place.rows_joined((out_a, out_b), layer_got)
    part, d2, e2, dq2, dkv, terms2 = cross_backward(
        d3, h2, part, other, norms, nums, kv, kvt, q2, qt2, ot2, lse2, w_cross, layer_got
    )
    other = place.swap_core(part)
    g_cross = attention_grads(place, et, dkv, ct, dq2, ot2, e2)
    came_cross = leave_plane(place, g_cross) if place.fast else None
    keep, send = encoder_grad(dkv, w_cross, (g_cross[0],))
    passed = pass_on(g_units, came_units, (keep,)) if place.fast else ()
    encoder_blocks = finish_encoder(keep, place.swap_core(send), frames, passed)
    encoder_got = place.rows_sent(encoder_blocks)
    held = encoder_blocks
    if place.fast:
        onward_units = cross_plane(place, passed)
        passed = pass_on(g_cross, came_cross, encoder_blocks)
        onward_cross = cross_plane(place, passed)
        g_units = units_sum(g_units, came_units, onward_units, passed)
        held = (g_units,)
    part, d1, e1, dqk, dv, terms1 = self_backward(
        d2, h1, part, other, norms, nums, qkv, qt, kt, ot1, lse1, w_self, held
    )
    other = place.swap_core(part)
    g_self = attention_grads(place, at, dqk, at, dv, ot1, e1)
    held = ()
    if place.fast:
        came_self = leave_plane(place, g_self)
        cross_blocks = column_blocks(
            g_cross, came_cross, onward_cross, True, (), [g_self[0]] + encoder_got
        )
        held = (cross_blocks[0],)
        s_cross = scatter_column(place, cross_blocks[0], place.swap_core(cross_blocks[1]))
    grad_encoder = place.rows_joined(encoder_blocks, encoder_got).astype(F32)
    terms, out_a, out_b = finish_hidden(
        d1, hidden, part, other, norms, terms1, terms2, terms3, held
    )
    hidden_got = place.rows_sent((out_a, out_b))
    grad_hidden = place.rows_joined((out_a, out_b), hidden_got).astype(F32)
    s_up, s_down = scatter_units(place, g_units, (terms,))

    few = D // (place.dp * place.mp)
    if place.fast:
        onward_self = cross_plane(place, pass_on(g_self, came_self, (s_down,)))
        terms = terms + place.swap_xy(terms, 1)
        blocks = column_blocks(
            g_self, came_self, onward_self, False, (terms, place.swap_xy(terms, 2)), (s_up,)
        )
        g_qkv, g_out, g_gain, g_bias = finish_self(place.column_back(blocks), blocks[3], few)
        g_ckv, g_cq, g_cout = finish_cross(s_cross)
        g_qkv = g_qkv.transpose(1, 0, 2)
    else:
        s_cross = sum_plain(place, g_cross, True)
        s_self = sum_plain(place, g_self, True)
        terms = jnp.where(place.core == 0, terms, 0.0)
        terms = lax.psum(terms, AXES)
        shares = lax.dynamic_slice_in_dim(terms, (place.z * place.dp + place.d) * few, few, 1)
        g_gain, g_bias = shares[:4], shares[4:]
        g_qkv, g_out = s_self[:, : 3 * QUARTER], from_quarters(s_self[:, 3 * QUARTER :])
        g_ckv, g_cq = s_cross[:, :HALF], s_cross[:, HALF : 3 * QUARTER]
        g_cout = from_quarters(s_cross[:, 3 * QUARTER :])
    return (
        layer_out,
        grad_hidden,
        grad_encoder,
        g_qkv.reshape(rows, 3, QUARTER),
        g_out,
        g_cq,
        g_ckv.reshape(rows, 2, QUARTER),
        g_cout,
        s_up,
        s_down,
        g_gain,
        g_bias,
    )


def solution(mesh):
    dp, mp = mesh.shape["dp"], mesh.shape["mp"]
    finer = Mesh(mesh.devices.reshape(dp // 2, 2, mp), AXES)
    both = ("xy", "core")
    rows = P(None, both, None, "mp")
    columns = P(both, None, "mp")
    pairs = P(both, "mp")
    units = P(("mp",) + both, None)
    each = P(None, both)
    return jax.shard_map(
        partial(per_device, dp, mp),
        mesh=finer,
        in_specs=(
            rows,
            P(None, both, None, None),
            rows,
            columns,
            units,
            pairs,
            columns,
            units,
            pairs,
            units,
            P(None, "mp"),
            P(None, "mp"),
            each,
            each,
            each,
            P(),
        ),
        out_specs=(
            rows,
            rows,
            rows,
            columns,
            units,
            pairs,
            columns,
            units,
            pairs,
            units,
            P(None, ("mp",) + both),
            P(None, ("mp",) + both),
        ),
        check_vma=False,
    )
```

profile of v0, /device:TPU:1, one launch (start us, length us, event | category | flops | bytes accessed | tf_op | source)
XLA Modules:
  0.0 340.1 jit_solution(5080826275399878325)
XLA Ops:
  11.6 5.6 %collective-permute-start.3 = (bf16[96,1536]{1,0:T(8,128)(2,1)S(1)}, bf16[96,1536]{1,0:T(8,128)(2,1)S(1)}, u32[]{:S(2)}, u32[]{:S(2)}) collective-permute-start(bf16[96,1536]{1,0:T(8,128)(2,1)S(1)} %shard_map.247.refs_4_.refs_3_), channel_id=1, source_target_pairs={{2,4},{3,5},{4,2},{5,3},{10,12},{11,13},{12,10},{13,11},{18,20},{1... | collective-permute-start | bytes 884744 | tf_op jit(solution)/shard_map/ppermute | solution.py:133
  21.0 6.0 %constant_dynamic-slice_fusion = bf16[1,1,1500,768]{3,0,2,1:T(2,128)(2,1)S(1)} fusion(bf16[2,1,1500,768]{3,0,2,1:T(2,128)(2,1)} %param.17, s32[]{:T(128)S(6)} %select_n.125), kind=kLoop, calls=%fused_computation.40 | loop fusion | bytes 4608004 | tf_op jit(solution)/shard_map/jit(dynamic_index_in_dim)/dynamic_slice | solution.py:1561
  30.5 5.6 %collective-permute-done.3.refs_3_ = bf16[96,1536]{1,0:T(8,128)(2,1)S(1)} collective-permute-done((bf16[96,1536]{1,0:T(8,128)(2,1)S(1)}, bf16[96,1536]{1,0:T(8,128)(2,1)S(1)}, u32[]{:S(2)}, u32[]{:S(2)}) %collective-permute-start.3) | collective-permute-done | bytes 294944 | tf_op jit(solution)/shard_map/ppermute | solution.py:133
  36.1 7.8 %collective-permute-done.1.refs_1_ = bf16[96,1536]{1,0:T(8,128)(2,1)} collective-permute-done((bf16[96,1536]{1,0:T(8,128)(2,1)S(1)}, bf16[96,1536]{1,0:T(8,128)(2,1)}, u32[]{:S(2)}, u32[]{:S(2)}) %collective-permute-start.1) | collective-permute-done | bytes 294944 | tf_op jit(solution)/shard_map/ppermute | solution.py:133
  55.7 6.4 %collective-permute-done.5 = bf16[224,448]{1,0:T(8,128)(2,1)S(1)} collective-permute-done((bf16[224,448]{1,0:T(8,128)(2,1)S(1)}, bf16[224,448]{1,0:T(8,128)(2,1)S(1)}, u32[]{:S(2)}, u32[]{:S(2)}) %collective-permute-start.5) | collective-permute-done | bytes 200736 | tf_op jit(solution)/shard_map/ppermute | solution.py:133
  71.5 10.7 %collective-permute-done.8.refs_4_.refs_2_.refs_8_.refs_13_.refs_12_ = bf16[2,2,192,768]{3,2,1,0:T(8,128)(2,1)} collective-permute-done((bf16[2,2,192,768]{3,2,1,0:T(8,128)(2,1)}, bf16[2,2,192,768]{3,2,1,0:T(8,128)(2,1)}, u32[]{:S(2)}, u32[]{:S(2)}) %collective-permute-start.8) | collective-permute-done | bytes 1179680 | tf_op jit(solution)/shard_map/ppermute | solution.py:133
  86.2 9.1 %collective-permute-done.14.refs_2_ = bf16[192,768]{1,0:T(8,128)(2,1)S(1)} collective-permute-done((bf16[192,768]{1,0:T(8,128)(2,1)S(1)}, bf16[192,768]{1,0:T(8,128)(2,1)S(1)}, u32[]{:S(2)}, u32[]{:S(2)}) %collective-permute-start.14) | collective-permute-done | bytes 294944 | tf_op jit(solution)/shard_map/ppermute | solution.py:133
  103.3 7.6 %shard_map.253 = (bf16[448,768]{1,0:T(8,128)(2,1)S(1)}, bf16[768,448]{1,0:T(8,128)(2,1)S(1)}, bf16[448,1152]{1,0:T(8,128)(2,1)S(1)}, bf16[384,448]{1,0:T(8,128)(...) custom-call(bf16[448,768]{1,0:T(8,128)(2,1)S(1)} %get-tuple-element.107.refs_0_.refs_, ...), custom_call_target="tpu_custom_call" | custom-call | flops 11500000256 | bytes 8886784 | tf_op jit(solution)/shard_map/pallas_call | solution.py:79
  117.5 4.6 %shard_map.254 = (bf16[1536,768]{1,0:T(8,128)(2,1)S(1)}, bf16[768,1536]{1,0:T(8,128)(2,1)S(1)}) custom-call(bf16[1536,768]{1,0:T(8,128)(2,1)S(1)} %pad.4.refs_0_, bf16[2,2,192,768]{3,2,1,0:T(8,128)(2,1)} %shard_map.248.refs_3_.refs_1_.refs_7_.refs_12_.refs_11_, bf16[2,2,192,768]{3,2,1,0:T(8,128)(2,1)} %collective-permute-done.8.refs_4_.refs_2_.refs_8_.refs_13_.refs_12_, ...), custom_call_target="tpu_custom_call" | custom-call | flops 6899999744 | bytes 11796480 | tf_op jit(solution)/shard_map/pallas_call | solution.py:79
  122.1 11.3 %shard_map.255 = (bf16[448,768]{1,0:T(8,128)(2,1)S(1)}, f32[448,768]{1,0:T(8,128)S(1)}, bf16[768,448]{1,0:T(8,128)(2,1)S(1)}, bf16[448,384]{1,0:T(8,128)(2,1)S(1...) custom-call(bf16[448,768]{1,0:T(8,128)(2,1)S(1)} %get-tuple-element.107.refs_0_.refs_1_, ...), custom_call_target="tpu_custom_call" | custom-call | flops 11500000256 | bytes 15325696 | tf_op jit(solution)/shard_map/pallas_call | solution.py:79
  134.5 7.4 %collective-permute-done.19.refs_6_.refs_9_ = bf16[2,2,192,768]{3,2,1,0:T(8,128)(2,1)S(1)} collective-permute-done((bf16[2,2,192,768]{3,2,1,0:T(8,128)(2,1)S(1)}, bf16[2,2,192,768]{3,2,1,0:T(8,128)(2,1)S(1)}, u32[]{:S(2)}, u32[]{:S(2)}) %collective-permute-start.19) | collective-permute-done | bytes 1179680 | tf_op jit(solution)/shard_map/ppermute | solution.py:133
  149.7 7.1 %collective-permute-done.23 = bf16[192,448]{1,0:T(8,128)(2,1)S(1)} collective-permute-done((bf16[192,448]{1,0:T(8,128)(2,1)S(1)}, bf16[192,448]{1,0:T(8,128)(2,1)S(1)}, u32[]{:S(2)}, u32[]{:S(2)}) %collective-permute-start.23) | collective-permute-done | bytes 172064 | tf_op jit(solution)/shard_map/ppermute | solution.py:133
  157.3 5.5 %shard_map.256 = (bf16[448,768]{1,0:T(8,128)(2,1)S(1)}, f32[448,768]{1,0:T(8,128)S(1)}, bf16[768,448]{1,0:T(8,128)(2,1)S(1)}, bf16[448,1536]{1,0:T(8,128)(2,1)S(1)}, bf16[1536,448]{1,0:T(8,128)(2,1)S(1)}) custom-call(f32[448,768]{1,0:T(8,128)S(1)} %get-tuple-element.114.refs_0_.refs_1_, bf16[448,768]{1,0:T(8,128)(2,1)S(1)} %get-tuple-element.115.refs_1_.refs_2_, ...), custom_call_target="tpu_custom_call" | custom-call | flops 10350000128 | bytes 13000704 | tf_op jit(solution)/shard_map/pallas_call | solution.py:79
  168.6 6.0 %shard_map.259 = (bf16[448,768]{1,0:T(8,128)(2,1)S(1)}, f32[448,768]{1,0:T(8,128)S(1)}, bf16[448,768]{1,0:T(8,128)(2,1)S(1)}, bf16[448,1536]{1,0:T(8,128)(2,1)S(...) custom-call(f32[448,768]{1,0:T(8,128)S(1)} %get-tuple-element.116.refs_0_.refs_1_, ...), custom_call_target="tpu_custom_call" | custom-call | flops 11500000256 | bytes 14043136 | tf_op jit(solution)/shard_map/pallas_call | solution.py:79
  178.8 4.4 %shard_map.261 = (bf16[2,4,192,384]{3,2,1,0:T(8,128)(2,1)}, bf16[2,4,192,384]{3,2,1,0:T(8,128)(2,1)S(1)}, bf16[2,4,96,768]{3,2,1,0:T(8,128)(2,1)}, bf16[2,4,96,768]{3,2,1,0:T(8,128)(2,1)S(1)}) custom-call(bf16[768,448]{1,0:T(8,128)(2,1)S(1)} %get-tuple-element.137.refs_0_, bf16[448,1536]{1,0:T(8,128)(2,1)S(1)} %get-tuple-element.138.refs_1_, ...), custom_call_target="tpu_custom_call" | custom-call | flops 6899999744 | bytes 8847360 | tf_op jit(solution)/shard_map/pallas_call | solution.py:79
  186.3 21.9 %shard_map.260 = (bf16[448,768]{1,0:T(8,128)(2,1)}, f32[448,768]{1,0:T(8,128)S(1)}, bf16[448,768]{1,0:T(8,128)(2,1)S(1)}, bf16[448,384]{1,0:T(8,128)(2,1)S(1)}, ...) custom-call(f32[448,768]{1,0:T(8,128)S(1)} %get-tuple-element.124.refs_0_, ...), custom_call_target="tpu_custom_call" | custom-call | flops 25300000768 | bytes 20099584 | tf_op jit(solution)/shard_map/pallas_call | solution.py:79
  214.5 4.1 %shard_map.263 = (bf16[384,1536]{1,0:T(8,128)(2,1)S(1)}, bf16[384,1536]{1,0:T(8,128)(2,1)}) custom-call(bf16[1536,768]{1,0:T(8,128)(2,1)S(1)} %copy-done.38, bf16[2,2,192,768]{3,2,1,0:T(8,128)(2,1)} %shard_map.248.refs_3_.refs_1_.refs_7_.refs_12_.refs_11_, bf16[2,2,192,768]{3,2,1,0:T(8,128)(2,1)} %collective-permute-done.8.refs_4_.refs_2_.refs_8_.refs_13_.refs_12_, ...), custom_call_target="tpu_custom_call" | custom-call | flops 4024999936 | bytes 9437184 | tf_op jit(solution)/shard_map/pallas_call | solution.py:79
  230.8 3.9 %collective-permute-done.35.refs_3_.refs_4_ = bf16[2,192,768]{2,1,0:T(8,128)(2,1)S(1)} collective-permute-done((bf16[2,192,768]{2,1,0:T(8,128)(2,1)}, bf16[2,192,768]{2,1,0:T(8,128)(2,1)S(1)}, u32[]{:S(2)}, u32[]{:S(2)}) %collective-permute-start.35) | collective-permute-done | bytes 589856 | tf_op jit(solution)/shard_map/ppermute | solution.py:133
  234.6 4.7 %collective-permute-start.41 = (bf16[192,1500]{1,0:T(8,128)(2,1)}, bf16[192,1500]{1,0:T(8,128)(2,1)}, u32[]{:S(2)}, u32[]{:S(2)}) collective-permute-start(bf16[192,1500]{1,0:T(8,128)(2,1)} %get-tuple-element.158.refs_5_), channel_id=1, source_target_pairs={{0,1},{1,0},{2,5},{3,4},{4,3},{5,2},{6,7},{7,6},{8,9},{9,8},{10,13... | collective-permute-start | bytes 1728008 | tf_op jit(solution)/shard_map/ppermute | solution.py:133
  242.5 4.9 %collective-permute-done.32.refs_2_ = bf16[4,192,384]{2,1,0:T(8,128)(2,1)S(1)} collective-permute-done((bf16[4,192,384]{2,1,0:T(8,128)(2,1)S(1)}, bf16[4,192,384]{2,1,0:T(8,128)(2,1)S(1)}, u32[]{:S(2)}, u32[]{:S(2)}) %collective-permute-start.32) | collective-permute-done | bytes 589856 | tf_op jit(solution)/shard_map/ppermute | solution.py:133
  261.5 11.8 %shard_map.268 = (bf16[448,768]{1,0:T(8,128)(2,1)S(1)}, f32[448,768]{1,0:T(8,128)S(1)}, bf16[448,768]{1,0:T(8,128)(2,1)S(1)}, bf16[448,768]{1,0:T(8,128)(2,1)S(1...) custom-call(f32[448,768]{1,0:T(8,128)S(1)} %copy-done.48, f32[448,768]{1,0:T(8,128)S(1)} %copy-done.44, ...), custom_call_target="tpu_custom_call" | custom-call | flops 13799999488 | bytes 14742016 | tf_op jit(solution)/shard_map/pallas_call | solution.py:79
  290.8 4.1 %collective-permute-start.43 = (bf16[192,448]{1,0:T(8,128)(2,1)S(1)}, bf16[192,448]{1,0:T(8,128)(2,1)S(1)}, u32[]{:S(2)}, u32[]{:S(2)}) collective-permute-start(bf16[192,448]{1,0:T(8,128)(2,1)S(1)} %get-tuple-element.172), channel_id=1, source_target_pairs={{0,1},{1,0},{2,5},{3,4},{4,3},{5,2},{6,7},{7,6},{8,9},{9,8},{10,13... | collective-permute-start | bytes 516104 | tf_op jit(solution)/shard_map/ppermute | solution.py:133
  303.8 8.3 %collective-permute-done.42 = bf16[192,448]{1,0:T(8,128)(2,1)S(1)} collective-permute-done((bf16[192,448]{1,0:T(8,128)(2,1)S(1)}, bf16[192,448]{1,0:T(8,128)(2,1)S(1)}, u32[]{:S(2)}, u32[]{:S(2)}) %collective-permute-start.42) | collective-permute-done | bytes 172064 | tf_op jit(solution)/shard_map/ppermute | solution.py:133
  326.0 6.2 %collective-permute-done.54.refs_3_ = bf16[112,768]{1,0:T(8,128)(2,1)S(1)} collective-permute-done((bf16[112,768]{1,0:T(8,128)(2,1)S(1)}, bf16[112,768]{1,0:T(8,128)(2,1)S(1)}, u32[]{:S(2)}, u32[]{:S(2)}) %collective-permute-start.54) | collective-permute-done | bytes 172064 | tf_op jit(solution)/shard_map/ppermute | solution.py:133
  (296 shorter events, 150.1 us)
Async XLA Ops:
  7.2 289.7 %reduce-scatter.3.cloned.1.call-start = ((), (), s32[]{:S(2)}) async-start(), calls=%async_computation.2 | async-start | bytes 1474560 | tf_op jit(solution)/shard_map/reduce_scatter | solution.py:456
  11.6 24.4 %collective-permute-start.3 = (bf16[96,1536]{1,0:T(8,128)(2,1)S(1)}, bf16[96,1536]{1,0:T(8,128)(2,1)S(1)}, u32[]{:S(2)}, u32[]{:S(2)}) collective-permute-start(bf16[96,1536]{1,0:T(8,128)(2,1)S(1)} %shard_map.247.refs_4_.refs_3_), channel_id=1, source_target_pairs={{2,4},{3,5},{4,2},{5,3},{10,12},{11,13},{12,10},{13,11},{18,20},{1... | collective-permute-start | bytes 884744 | tf_op jit(solution)/shard_map/ppermute | solution.py:133
  17.3 26.5 %collective-permute-start.1 = (bf16[96,1536]{1,0:T(8,128)(2,1)S(1)}, bf16[96,1536]{1,0:T(8,128)(2,1)}, u32[]{:S(2)}, u32[]{:S(2)}) collective-permute-start(bf16[96,1536]{1,0:T(8,128)(2,1)S(1)} %shard_map.247.refs_4_.refs_3_), channel_id=1, source_target_pairs={{0,2},{1,3},{2,6},{3,7},{4,0},{5,1},{6,4},{7,5},{8,10},{9,11},{10,... | collective-permute-start | bytes 884744 | tf_op jit(solution)/shard_map/ppermute | solution.py:133
  18.7 25.1 %collective-permute-start = (bf16[96,1536]{1,0:T(8,128)(2,1)S(1)}, bf16[96,1536]{1,0:T(8,128)(2,1)}, u32[]{:S(2)}, u32[]{:S(2)}) collective-permute-start(bf16[96,1536]{1,0:T(8,128)(2,1)S(1)} %shard_map.247.refs_4_.refs_3_), channel_id=1, source_target_pairs={{0,1},{1,0},{2,5},{3,4},{4,3},{5,2},{6,7},{7,6},{8,9},{9,8},{10,13... | collective-permute-start | bytes 884744 | tf_op jit(solution)/shard_map/ppermute | solution.py:133
  29.1 69.9 %collective-permute-start.12 = (bf16[1500,768]{1,0:T(8,128)(2,1)S(1)}, bf16[1500,768]{1,0:T(8,128)(2,1)}, u32[]{:S(2)}, u32[]{:S(2)}) collective-permute-start(bf16[1500,768]{1,0:T(8,128)(2,1)S(1)} %bitcast.75), channel_id=1, source_target_pairs={{0,4},{1,5},{6,2},{7,3},{8,12},{9,13},{14,10},{15,11},{16,20},{17,... | collective-permute-start | bytes 6912008 | tf_op jit(solution)/shard_map/ppermute | solution.py:133
  46.3 22.1 %collective-permute-start.9 = (bf16[2,2,192,768]{3,2,1,0:T(8,128)(2,1)}, bf16[2,2,192,768]{3,2,1,0:T(8,128)(2,1)}, u32[]{:S(2)}, u32[]{:S(2)}) collective-permute-start(bf16[2,2,192,768]{3,2,1,0:T(8,128)(2,1)} %shard_map.248.refs_3_.refs_1_.refs_7_.refs_12_.refs_11_), channel_id=1, source_target_pairs={{0,16},{1,17},{2,18},{3,19},{4,20},{5,21},{6,22},{7,23},{8,24},{9,... | collective-permute-start | bytes 3538952 | tf_op jit(solution)/shard_map/ppermute | solution.py:133
  53.8 28.4 %collective-permute-start.8 = (bf16[2,2,192,768]{3,2,1,0:T(8,128)(2,1)}, bf16[2,2,192,768]{3,2,1,0:T(8,128)(2,1)}, u32[]{:S(2)}, u32[]{:S(2)}) collective-permute-start(bf16[2,2,192,768]{3,2,1,0:T(8,128)(2,1)} %shard_map.248.refs_3_.refs_1_.refs_7_.refs_12_.refs_11_), channel_id=1, source_target_pairs={{0,8},{1,9},{2,10},{3,11},{4,12},{5,13},{6,14},{7,15},{8,0},{9,1},... | collective-permute-start | bytes 3538952 | tf_op jit(solution)/shard_map/ppermute | solution.py:133
  70.3 27.7 %collective-permute-start.11 = (bf16[2,192,768]{2,1,0:T(8,128)(2,1)}, bf16[2,192,768]{2,1,0:T(8,128)(2,1)}, u32[]{:S(2)}, u32[]{:S(2)}) collective-permute-start(bf16[2,192,768]{2,1,0:T(8,128)(2,1)} %slice_bitcast_fusion.2), channel_id=1, source_target_pairs={{0,8},{1,9},{2,10},{3,11},{4,12},{5,13},{6,14},{7,15},{8,0},{9,1},... | collective-permute-start | bytes 1769480 | tf_op jit(solution)/shard_map/ppermute | solution.py:133
  114.8 27.1 %collective-permute-start.19 = (bf16[2,2,192,768]{3,2,1,0:T(8,128)(2,1)S(1)}, bf16[2,2,192,768]{3,2,1,0:T(8,128)(2,1)S(1)}, u32[]{:S(2)}, u32[]{:S(2)}) collective-permute-start(bf16[2,2,192,768]{3,2,1,0:T(8,128)(2,1)S(1)} %shard_map.252.refs_9_.refs_4_.refs_7_), channel_id=1, source_target_pairs={{0,16},{1,17},{2,18},{3,19},{4,20},{5,21},{6,22},{7,23},{8,24},{9,... | collective-permute-start | bytes 3538952 | tf_op jit(solution)/shard_map/ppermute | solution.py:133
  116.2 27.3 %collective-permute-start.18 = (bf16[2,2,192,768]{3,2,1,0:T(8,128)(2,1)S(1)}, bf16[2,2,192,768]{3,2,1,0:T(8,128)(2,1)S(1)}, u32[]{:S(2)}, u32[]{:S(2)}) collective-permute-start(bf16[2,2,192,768]{3,2,1,0:T(8,128)(2,1)S(1)} %shard_map.252.refs_9_.refs_4_.refs_7_), channel_id=1, source_target_pairs={{0,8},{1,9},{2,10},{3,11},{4,12},{5,13},{6,14},{7,15},{8,0},{9,1},... | collective-permute-start | bytes 3538952 | tf_op jit(solution)/shard_map/ppermute | solution.py:133
  133.5 23.3 %collective-permute-start.17 = (bf16[448,768]{1,0:T(8,128)(2,1)S(1)}, bf16[448,768]{1,0:T(8,128)(2,1)S(1)}, u32[]{:S(2)}, u32[]{:S(2)}) collective-permute-start(bf16[448,768]{1,0:T(8,128)(2,1)S(1)} %get-tuple-element.115.refs_1_.refs_2_), channel_id=1, source_target_pairs={{0,4},{1,5},{2,6},{3,7},{4,0},{5,1},{6,2},{7,3},{8,12},{9,13},{10,... | collective-permute-start | bytes 2064392 | tf_op jit(solution)/shard_map/ppermute | solution.py:133
  183.1 37.9 %collective-permute-start.30 = (bf16[2,4,192,384]{3,2,1,0:T(8,128)(2,1)}, bf16[2,4,192,384]{3,2,1,0:T(8,128)(2,1)S(1)}, u32[]{:S(2)}, u32[]{:S(2)}) collective-permute-start(bf16[2,4,192,384]{3,2,1,0:T(8,128)(2,1)} %get-tuple-element.142), channel_id=1, source_target_pairs={{0,8},{1,9},{2,10},{3,11},{4,12},{5,13},{6,14},{7,15},{8,0},{9,1},... | collective-permute-start | bytes 3538952 | tf_op jit(solution)/shard_map/ppermute | solution.py:133
  183.4 37.6 %collective-permute-start.31 = (bf16[2,4,96,768]{3,2,1,0:T(8,128)(2,1)}, bf16[2,4,96,768]{3,2,1,0:T(8,128)(2,1)}, u32[]{:S(2)}, u32[]{:S(2)}) collective-permute-start(bf16[2,4,96,768]{3,2,1,0:T(8,128)(2,1)} %get-tuple-element.144), channel_id=1, source_target_pairs={{0,16},{1,17},{2,18},{3,19},{4,20},{5,21},{6,22},{7,23},{8,24},{9,... | collective-permute-start | bytes 3538952 | tf_op jit(solution)/shard_map/ppermute | solution.py:133
  219.7 19.7 %collective-permute-start.34 = (bf16[2,192,768]{2,1,0:T(8,128)(2,1)}, bf16[2,192,768]{2,1,0:T(8,128)(2,1)S(1)}, u32[]{:S(2)}, u32[]{:S(2)}) collective-permute-start(bf16[2,192,768]{2,1,0:T(8,128)(2,1)} %copy-done.12), channel_id=1, source_target_pairs={{0,8},{1,9},{2,10},{3,11},{4,12},{5,13},{6,14},{7,15},{8,0},{9,1},... | collective-permute-start | bytes 1769480 | tf_op jit(solution)/shard_map/ppermute | solution.py:133
  224.0 23.3 %collective-permute-start.32 = (bf16[4,192,384]{2,1,0:T(8,128)(2,1)S(1)}, bf16[4,192,384]{2,1,0:T(8,128)(2,1)S(1)}, u32[]{:S(2)}, u32[]{:S(2)}) collective-permute-start(bf16[4,192,384]{2,1,0:T(8,128)(2,1)S(1)} %get-tuple-element.151.refs_2_), channel_id=1, source_target_pairs={{0,16},{1,17},{2,18},{3,19},{4,20},{5,21},{6,22},{7,23},{8,24},{9,... | collective-permute-start | bytes 1769480 | tf_op jit(solution)/shard_map/ppermute | solution.py:133
  224.9 23.1 %collective-permute-start.33 = (bf16[4,96,768]{2,1,0:T(8,128)(2,1)S(1)}, bf16[4,96,768]{2,1,0:T(8,128)(2,1)S(1)}, u32[]{:S(2)}, u32[]{:S(2)}) collective-permute-start(bf16[4,96,768]{2,1,0:T(8,128)(2,1)S(1)} %get-tuple-element.152.refs_3_), channel_id=1, source_target_pairs={{0,8},{1,9},{2,10},{3,11},{4,12},{5,13},{6,14},{7,15},{8,0},{9,1},... | collective-permute-start | bytes 1769480 | tf_op jit(solution)/shard_map/ppermute | solution.py:133
  225.7 26.7 %collective-permute-start.29 = (bf16[448,768]{1,0:T(8,128)(2,1)}, bf16[448,768]{1,0:T(8,128)(2,1)}, u32[]{:S(2)}, u32[]{:S(2)}) collective-permute-start(bf16[448,768]{1,0:T(8,128)(2,1)} %get-tuple-element.131.refs_2_), channel_id=1, source_target_pairs={{0,4},{1,5},{2,6},{3,7},{4,0},{5,1},{6,2},{7,3},{8,12},{9,13},{10,... | collective-permute-start | bytes 2064392 | tf_op jit(solution)/shard_map/ppermute | solution.py:133
  234.6 44.0 %collective-permute-start.41 = (bf16[192,1500]{1,0:T(8,128)(2,1)}, bf16[192,1500]{1,0:T(8,128)(2,1)}, u32[]{:S(2)}, u32[]{:S(2)}) collective-permute-start(bf16[192,1500]{1,0:T(8,128)(2,1)} %get-tuple-element.158.refs_5_), channel_id=1, source_target_pairs={{0,1},{1,0},{2,5},{3,4},{4,3},{5,2},{6,7},{7,6},{8,9},{9,8},{10,13... | collective-permute-start | bytes 1728008 | tf_op jit(solution)/shard_map/ppermute | solution.py:133
  239.4 42.1 %collective-permute-start.40 = (bf16[192,1500]{1,0:T(8,128)(2,1)}, bf16[192,1500]{1,0:T(8,128)(2,1)}, u32[]{:S(2)}, u32[]{:S(2)}) collective-permute-start(bf16[192,1500]{1,0:T(8,128)(2,1)} %get-tuple-element.157.refs_4_), channel_id=1, source_target_pairs={{2,4},{3,5},{4,2},{5,3},{10,12},{11,13},{12,10},{13,11},{18,20},{1... | collective-permute-start | bytes 1728008 | tf_op jit(solution)/shard_map/ppermute | solution.py:133
  247.4 30.1 %collective-permute-start.38 = (bf16[192,768]{1,0:T(8,128)(2,1)}, bf16[192,768]{1,0:T(8,128)(2,1)}, u32[]{:S(2)}, u32[]{:S(2)}) collective-permute-start(bf16[192,768]{1,0:T(8,128)(2,1)} %get-tuple-element.159.refs_6_), channel_id=1, source_target_pairs={{0,16},{1,17},{2,18},{3,19},{4,20},{5,21},{6,22},{7,23},{8,24},{9,... | collective-permute-start | bytes 884744 | tf_op jit(solution)/shard_map/ppermute | solution.py:133
  248.0 29.9 %collective-permute-start.39 = (bf16[192,768]{1,0:T(8,128)(2,1)}, bf16[192,768]{1,0:T(8,128)(2,1)}, u32[]{:S(2)}, u32[]{:S(2)}) collective-permute-start(bf16[192,768]{1,0:T(8,128)(2,1)} %get-tuple-element.160.refs_7_), channel_id=1, source_target_pairs={{0,8},{1,9},{2,10},{3,11},{4,12},{5,13},{6,14},{7,15},{8,0},{9,1},... | collective-permute-start | bytes 884744 | tf_op jit(solution)/shard_map/ppermute | solution.py:133
  252.4 69.2 %reduce-scatter.5.cloned.1.call-start = ((), (), s32[]{:S(2)}) async-start(), calls=%async_computation.3 | async-start | bytes 737280 | tf_op jit(solution)/shard_map/reduce_scatter | solution.py:1445
  277.5 21.1 %collective-permute-start.47 = (bf16[2,192,768]{2,1,0:T(8,128)(2,1)S(1)}, bf16[2,192,768]{2,1,0:T(8,128)(2,1)S(1)}, u32[]{:S(2)}, u32[]{:S(2)}) collective-permute-start(bf16[2,192,768]{2,1,0:T(8,128)(2,1)S(1)} %get-tuple-element.176), channel_id=1, source_target_pairs={{0,16},{1,17},{2,18},{3,19},{4,20},{5,21},{6,22},{7,23},{8,24},{9,... | collective-permute-start | bytes 1769480 | tf_op jit(solution)/shard_map/ppermute | solution.py:133
  277.9 20.7 %collective-permute-start.46 = (bf16[2,192,768]{2,1,0:T(8,128)(2,1)S(1)}, bf16[2,192,768]{2,1,0:T(8,128)(2,1)S(1)}, u32[]{:S(2)}, u32[]{:S(2)}) collective-permute-start(bf16[2,192,768]{2,1,0:T(8,128)(2,1)S(1)} %get-tuple-element.169.refs_6_), channel_id=1, source_target_pairs={{0,8},{1,9},{2,10},{3,11},{4,12},{5,13},{6,14},{7,15},{8,0},{9,1},... | collective-permute-start | bytes 1769480 | tf_op jit(solution)/shard_map/ppermute | solution.py:133
  (103 other events, 1034.5 us)
Sparse Core Ops, SparseCore 0:
  252.5 33.0 reduce-scatter.2
  288.3 24.5 reduce-scatter.4
where the time goes:
time: 345 us; the launch traced here: 340 us
  Pallas kernels  107 us (31%)
  waiting for transfers between devices  90.1 us (26%)
  starting transfers between devices  74 us (21%)
  local copies, waits for them, and re-layouts  41.1 us (12%)
  between operations  15.4 us (4%)
  other arithmetic  13 us (4%)
    pallas_call x31, Pallas kernels, run(): pl.pallas_call(whole, out_shape=tuple(outs), in_specs=[SMEM] * len(smem)...  107 us
    ppermute x56, waiting for transfers between devices, move(): return lax.ppermute(value, AXES, pairs)  90 us
    ppermute x56, starting transfers between devices, move(): return lax.ppermute(value, AXES, pairs)  73.9 us
    unnamed x139, local copies, waits for them, and re-layouts  28 us
  transfers between devices with their start and end apart: 58, of which 20 were waited for; matrix products, arithmetic and copies ran while one was open for 6% of the time, Pallas kernels for 27%

commit v1 on v0

--- a/solution.py
+++ b/solution.py
@@ -20,6 +20,7 @@
 VMEM = pl.BlockSpec(memory_space=pltpu.VMEM)
 SMEM = pl.BlockSpec(memory_space=pltpu.SMEM)
 ANY = pl.BlockSpec(memory_space=pl.ANY)
+HBM = pl.BlockSpec(memory_space=pltpu.HBM)
 
 
 def mm(left, right):
@@ -75,7 +76,7 @@
             copies.wait()
         body(*ins, *rest)
 
-    place = ANY if staged else VMEM
+    place = HBM if staged else VMEM
     return pl.pallas_call(
         whole,
         out_shape=tuple(outs),
@@ -349,6 +350,7 @@
         [shaped((rows, 2 * D))],
         vmem=[self_qkv.transpose(1, 0, 2), self_out, cross_kv.reshape(rows, -1), cross_q, cross_out],
         micros=2,
+        staged=True,
     )[0]
 
 
@@ -451,56 +453,18 @@
     return [up, down.transpose(1, 0, 3, 2, 4).reshape(2 * D, D)]
 
 
-def scatter_units(place, grads, after=()):
-    axes = "mp" if place.fast else CHIPS
-    total = lax.psum_scatter(grads, axes, scatter_dimension=0, tiled=False)
+def scatter_units(place, grads):
+    total = lax.psum_scatter(grads, CHIPS, scatter_dimension=0, tiled=False)
     rows = total.shape[0] // 2
-    if not place.fast:
-        kept = lax.dynamic_slice_in_dim(total, place.core * rows, rows, 0)
-        sent = lax.dynamic_slice_in_dim(total[:, :HALF], (1 - place.core) * rows, rows, 0)
-        came = place.swap_core(sent)
-        kept = kept[:, :HALF]
-        first = place.core == 0
-        both = jnp.stack([jnp.where(first, kept, came), jnp.where(first, came, kept)])
-        both = both.reshape(2, rows, place.chips, rows).transpose(1, 2, 0, 3).reshape(rows, D)
-        down = jnp.concatenate([total[:rows, HALF:], total[rows:, HALF:]], axis=1)
-        return both.astype(F32), down.astype(F32)
-
-    def cut(total_ref, kept_ref, sent_ref, down_ref):
-        core, _, _ = where_am_i()
-        mine = pl.ds(pl.multiple_of(core * rows, 16), rows)
-        theirs = pl.ds(pl.multiple_of((1 - core) * rows, 16), rows)
-        kept_ref[...] = total_ref[mine, 0:HALF]
-        sent_ref[...] = total_ref[theirs, 0:HALF]
-        down_ref[:, 0:HALF] = total_ref[0:rows, HALF:D].astype(F32)
-        down_ref[:, HALF:D] = total_ref[rows : 2 * rows, HALF:D].astype(F32)
-
-    kept, sent, down = run(
-        cut,
-        [shaped((rows, HALF)), shaped((rows, HALF)), shaped((rows, D), F32)],
-        vmem=[total],
-        micros=1,
-        after=after,
-    )
-
-    def join(kept_ref, came_ref, up_ref, both):
-        core, _, _ = where_am_i()
-        both[core] = kept_ref[...]
-        both[1 - core] = came_ref[...]
-        blocks = []
-        for chip in range(place.chips):
-            for parity in range(2):
-                blocks.append(both[parity, :, chip * rows : (chip + 1) * rows].astype(F32))
-        up_ref[...] = jnp.concatenate(blocks, axis=1)
-
-    up = run(
-        join,
-        [shaped((rows, D), F32)],
-        vmem=[kept, place.swap_core(sent)],
-        scratch=[pltpu.VMEM((2, rows, HALF), BF)],
-        micros=1,
-    )[0]
-    return up, down
+    kept = lax.dynamic_slice_in_dim(total, place.core * rows, rows, 0)
+    sent = lax.dynamic_slice_in_dim(total[:, :HALF], (1 - place.core) * rows, rows, 0)
+    came = place.swap_core(sent)
+    kept = kept[:, :HALF]
+    first = place.core == 0
+    both = jnp.stack([jnp.where(first, kept, came), jnp.where(first, came, kept)])
+    both = both.reshape(2, rows, place.chips, rows).transpose(1, 2, 0, 3).reshape(rows, D)
+    down = jnp.concatenate([total[:rows, HALF:], total[rows:, HALF:]], axis=1)
+    return both.astype(F32), down.astype(F32)
 
 
 def spread(place, own):
@@ -757,7 +721,7 @@
         hbm=weights,
         scratch=[pltpu.VMEM((D, D), BF)],
         copies=4,
-        micros=6,
+        micros=2,
     )
 
 
@@ -842,7 +806,7 @@
             pltpu.VMEM((frames, length), F32),
         ],
         copies=4 + 16,
-        micros=10,
+        micros=4,
     )
 
 
@@ -1257,26 +1221,104 @@
     rows = grads[3].shape[2]
 
     def body(*refs):
-        ins, (out_ref, left, right, sems) = refs[:6], refs[6:]
+        ins, (kept_ref, sent_ref, left, right, blocks, sems) = refs[:6], refs[6:]
+        _, _, mp = where_am_i()
         copies = Copies(sems)
         for i, ref in enumerate(ins):
             target = (left if i < 3 else right).at[i % 3]
             copies.start(ref if i % 3 == 2 else ref.at[0], target)
         copies.wait()
         for z in range(4):
-            out_ref[z, :, 0:HALF] = add_up(*[left[i, z] for i in range(3)]).astype(BF)
+            blocks[z, :, 0:HALF] = add_up(*[left[i, z] for i in range(3)]).astype(BF)
             down = add_up(*[right[i, z] for i in range(3)]).astype(BF)
-            out_ref[z, 0:rows, HALF:D] = down[:, :HALF]
-            out_ref[z, rows : 2 * rows, HALF:D] = down[:, HALF:]
-
-    return run(
-        body,
-        [shaped((4, 2 * rows, D))],
+            blocks[z, 0:rows, HALF:D] = down[:, :HALF]
+            blocks[z, rows : 2 * rows, HALF:D] = down[:, HALF:]
+        for i in range(2):
+            kept_ref[i] = blocks[mp ^ (2 * i)]
+            sent_ref[i] = blocks[mp ^ (2 * i + 1)]
+
+    return run(
+        body,
+        [shaped((2, 2 * rows, D)), shaped((2, 2 * rows, D))],
         hbm=[grads[1], came[0], onward[0], grads[3], came[1], onward[1]],
-        scratch=[pltpu.VMEM((3, 4, 2 * rows, HALF), BF), pltpu.VMEM((3, 4, rows, D), BF)],
+        scratch=[
+            pltpu.VMEM((3, 4, 2 * rows, HALF), BF),
+            pltpu.VMEM((3, 4, rows, D), BF),
+            pltpu.VMEM((4, 2 * rows, D), BF),
+        ],
         copies=6,
         micros=3,
         after=after,
+    )
+
+
+def add_second(kept, came, after):
+    def body(kept_ref, came_ref, out_ref, held, sems):
+        copies = Copies(sems)
+        copies.start(kept_ref.at[1], held.at[0])
+        copies.start(came_ref.at[1], held.at[1])
+        copies.wait()
+        out_ref[...] = add_up(held[0], held[1]).astype(BF)
+
+    shape = kept.shape[1:]
+    return run(
+        body,
+        [shaped(shape)],
+        hbm=[kept, came],
+        scratch=[pltpu.VMEM((2,) + shape, BF)],
+        copies=2,
+        micros=1,
+        after=after,
+    )[0]
+
+
+def cut_units(kept, came, last, after):
+    rows = last.shape[0] // 2
+
+    def body(kept_ref, came_ref, last_ref, mine_ref, sent_ref, down_ref, held, sems):
+        core, _, _ = where_am_i()
+        copies = Copies(sems)
+        copies.start(kept_ref.at[0], held.at[0])
+        copies.start(came_ref.at[0], held.at[1])
+        copies.start(last_ref, held.at[2])
+        copies.wait()
+        mine = pl.ds(pl.multiple_of(core * rows, 16), rows)
+        theirs = pl.ds(pl.multiple_of((1 - core) * rows, 16), rows)
+        mine_ref[...] = add_up(*[held[i, mine, 0:HALF] for i in range(3)]).astype(BF)
+        sent_ref[...] = add_up(*[held[i, theirs, 0:HALF] for i in range(3)]).astype(BF)
+        down_ref[:, 0:HALF] = add_up(*[held[i, 0:rows, HALF:D] for i in range(3)])
+        down_ref[:, HALF:D] = add_up(*[held[i, rows : 2 * rows, HALF:D] for i in range(3)])
+
+    return run(
+        body,
+        [shaped((rows, HALF)), shaped((rows, HALF)), shaped((rows, D), F32)],
+        hbm=[kept, came, last],
+        scratch=[pltpu.VMEM((3, 2 * rows, D), BF)],
+        copies=3,
+        micros=1,
+        after=after,
+    )
+
+
+def join_units(place, kept, came):
+    rows = kept.shape[0]
+
+    def body(kept_ref, came_ref, up_ref, both):
+        core, _, _ = where_am_i()
+        both[core] = kept_ref[...]
+        both[1 - core] = came_ref[...]
+        blocks = []
+        for chip in range(place.chips):
+            for parity in range(2):
+                blocks.append(both[parity, :, chip * rows : (chip + 1) * rows].astype(F32))
+        up_ref[...] = jnp.concatenate(blocks, axis=1)
+
+    return run(
+        body,
+        [shaped((rows, D), F32)],
+        vmem=[kept, came],
+        scratch=[pltpu.VMEM((2, rows, HALF), BF)],
+        micros=1,
     )[0]
 
 
@@ -1370,7 +1412,7 @@
     return [place.swap_xy(onward[0], 2), place.swap_xy(onward[1], 1)]
 
 
-def column_blocks(grads, came, onward, swapped, norm_terms=(), after=()):
+def column_blocks(grads, came, onward, norm_terms=(), after=()):
     shape = onward[0].shape
     rows = shape[-2] // 2
     width = D
@@ -1417,19 +1459,13 @@
                     offset = (2 * core + hi) * QUARTER + (2 * xy + cs) * few
                     pick = jnp.where((feature == lane + offset) & (lane < few), 1.0, 0.0)
                     shards[2 * hi + cs, rows:] = mm(terms, pick.astype(BF)).astype(BF)
-        if swapped:
-            core, _, _ = where_am_i()
-            for hi in range(2):
-                outs[0][hi] = shards[2 * hi + core]
-                outs[1][hi] = shards[2 * hi + 1 - core]
-        else:
-            for k in range(4):
-                outs[k][...] = shards[slots[k]]
+        for k in range(4):
+            outs[k][...] = shards[slots[k]]
 
     ins = [grads[1], came[0], onward[0], grads[3], came[1], onward[1]]
     return run(
         body,
-        [shaped((2, rows, width))] * 2 if swapped else [shaped((rows + extra, width))] * 4,
+        [shaped((rows + extra, width))] * 4,
         vmem=list(norm_terms),
         hbm=ins,
         after=after,
@@ -1437,12 +1473,6 @@
         copies=6,
         micros=2,
     )
-
-
-def scatter_column(place, kept, came):
-    first = place.core == 0
-    both = jnp.concatenate([jnp.where(first, kept, came), jnp.where(first, came, kept)])
-    return lax.psum_scatter(both, "mp", scatter_dimension=0, tiled=False)
 
 
 def sum_plain(place, grads, attention):
@@ -1500,12 +1530,14 @@
     )
 
 
-def finish_cross(total):
-    rows = total.shape[0]
+def finish_cross(got, own, after=()):
+    rows = own.shape[0]
     few = rows // 4
 
-    def body(ref, kv_ref, q_ref, out_ref):
-        blocks, out = attention_outputs(ref[...].astype(F32), rows, few)
+    def body(a, b, c, d, own_ref, kv_ref, q_ref, out_ref):
+        home, _ = column_slots()
+        last = jnp.where(home, own_ref[...].astype(F32), d[...].astype(F32))
+        blocks, out = attention_outputs(add_up(a[...], b[...], c[...], last), rows, few)
         kv_ref[...] = jnp.concatenate(blocks[:2], axis=1)
         q_ref[...] = blocks[2]
         out_ref[...] = out
@@ -1513,9 +1545,37 @@
     return run(
         body,
         [shaped((rows, HALF), F32), shaped((rows, QUARTER), F32), shaped((few, D), F32)],
-        vmem=[total],
+        vmem=list(got) + [own],
         micros=1.5,
-    )
+        after=after,
+    )
+
+
+def join_rows(blocks, got, dtype, after=()):
+    width, rows = blocks[0].shape
+
+    def body(block_ref, first_ref, second_ref, out_ref):
+        home, _ = column_slots()
+        _, _, z = where_am_i()
+
+        @pl.when(home)
+        def _():
+            out_ref[z % 2] = block_ref[...].astype(dtype)
+
+        @pl.when(jnp.logical_not(home))
+        def _():
+            out_ref[z % 2] = first_ref[...].astype(dtype)
+
+        out_ref[(z + 1) % 2] = second_ref[...].astype(dtype)
+
+    joined = run(
+        body,
+        [shaped((2, width, rows), dtype)],
+        vmem=[blocks[0]] + list(got),
+        micros=2,
+        after=after,
+    )[0]
+    return joined[:, None].transpose(0, 1, 3, 2)
 
 
 def from_quarters(value):
@@ -1565,7 +1625,6 @@
         packed = pack_attention(place.column_out(shard), shard, (encoded,))
         w_self = w_cross = spread(place, packed)
         first = (shard,)
-        fc_in, packed = lax.optimization_barrier((fc_in, packed))
     else:
         quarter = lambda w: w.reshape(-1, 4, QUARTER).transpose(1, 0, 2).reshape(-1, QUARTER)
         flat = lambda w: w.reshape(rows, -1)
@@ -1591,7 +1650,7 @@
     )
     got = place.rows_in(blocks)
     if place.fast:
-        unit, got = lax.optimization_barrier((unit, got))
+        unit, packed = lax.optimization_barrier((unit, packed))
         stacked = stack_units(
             [unit] + [place.swap_z(unit, k) for k in (1, 2, 3)], tuple(w_self[3:5])
         )
@@ -1603,9 +1662,7 @@
     encoded = jnp.pad(encoded, ((0, padded - frames), (0, 0)))
 
     et = turn(encoded)
-    part1, at, qkv, qt, kt, ot1, lse1 = self_forward(
-        hidden, norms, nums, w_self, (et,) + ((stacked,) if place.fast else ())
-    )
+    part1, at, qkv, qt, kt, ot1, lse1 = self_forward(hidden, norms, nums, w_self, (et,))
     other1 = place.swap_core(part1)
     got = place.rows_in(turned_blocks(turned(cotangent), (at,)))
     kv, kvt = cross_memory(encoded, w_cross)
@@ -1639,8 +1696,9 @@
         onward_units = cross_plane(place, passed)
         passed = pass_on(g_cross, came_cross, encoder_blocks)
         onward_cross = cross_plane(place, passed)
-        g_units = units_sum(g_units, came_units, onward_units, passed)
-        held = (g_units,)
+        kept, sent = units_sum(g_units, came_units, onward_units, passed)
+        came_units = place.swap_z(sent, 1)
+        held = (kept,)
     part, d1, e1, dqk, dv, terms1 = self_backward(
         d2, h1, part, other, norms, nums, qkv, qt, kt, ot1, lse1, w_self, held
     )
@@ -1649,30 +1707,37 @@
     held = ()
     if place.fast:
         came_self = leave_plane(place, g_self)
+        second = add_second(kept, came_units, (g_self[0],))
+        last_units = place.swap_z(second, 2)
         cross_blocks = column_blocks(
-            g_cross, came_cross, onward_cross, True, (), [g_self[0]] + encoder_got
+            g_cross, came_cross, onward_cross, (), [second] + encoder_got
         )
+        cross_got = place.column_back(cross_blocks)
         held = (cross_blocks[0],)
-        s_cross = scatter_column(place, cross_blocks[0], place.swap_core(cross_blocks[1]))
-    grad_encoder = place.rows_joined(encoder_blocks, encoder_got).astype(F32)
     terms, out_a, out_b = finish_hidden(
         d1, hidden, part, other, norms, terms1, terms2, terms3, held
     )
     hidden_got = place.rows_sent((out_a, out_b))
-    grad_hidden = place.rows_joined((out_a, out_b), hidden_got).astype(F32)
-    s_up, s_down = scatter_units(place, g_units, (terms,))
 
     few = D // (place.dp * place.mp)
     if place.fast:
-        onward_self = cross_plane(place, pass_on(g_self, came_self, (s_down,)))
+        passed = pass_on(g_self, came_self, (terms,))
+        onward_self = cross_plane(place, passed)
+        grad_encoder = join_rows(encoder_blocks, encoder_got, F32, passed)
+        mine, sent, s_down = cut_units(kept, came_units, last_units, passed)
+        s_up = join_units(place, mine, place.swap_core(sent))
         terms = terms + place.swap_xy(terms, 1)
         blocks = column_blocks(
-            g_self, came_self, onward_self, False, (terms, place.swap_xy(terms, 2)), (s_up,)
+            g_self, came_self, onward_self, (terms, place.swap_xy(terms, 2)), (s_down,)
         )
         g_qkv, g_out, g_gain, g_bias = finish_self(place.column_back(blocks), blocks[3], few)
-        g_ckv, g_cq, g_cout = finish_cross(s_cross)
+        g_ckv, g_cq, g_cout = finish_cross(cross_got, cross_blocks[3], (blocks[0],))
+        grad_hidden = join_rows((out_a, out_b), hidden_got, F32, (blocks[0],))
         g_qkv = g_qkv.transpose(1, 0, 2)
     else:
+        s_up, s_down = scatter_units(place, g_units)
+        grad_encoder = place.rows_joined(encoder_blocks, encoder_got).astype(F32)
+        grad_hidden = place.rows_joined((out_a, out_b), hidden_got).astype(F32)
         s_cross = sum_plain(place, g_cross, True)
         s_self = sum_plain(place, g_self, True)
         terms = jnp.where(place.core == 0, terms, 0.0)

time: 345 us -> 337 us (0.977)
  waiting for transfers between devices: 90.1 us -> 105 us
  between operations: 15.4 us -> 1.87 us
  local copies, waits for them, and re-layouts: 41.1 us -> 30.2 us
  starting transfers between devices: 74 us -> 81.9 us
  other arithmetic: 13 us -> 6.25 us
    ppermute x56 -> x61, waiting for transfers between devices: 90 us -> 105 us  [move(): return lax.ppermute(value, AXES, pairs)]
    unnamed x139 -> x121, local copies, waits for them, and re-layouts: 28 us -> 17.7 us
    ppermute x56 -> x61, starting transfers between devices: 73.9 us -> 81.9 us  [move(): return lax.ppermute(value, AXES, pairs)]
    unnamed x3 -> x1, other arithmetic: 4.37 us -> 0.79 us
    pallas_call x31 -> x34, Pallas kernels: 107 us -> 108 us  [run(): pl.pallas_call(whole, out_shape=tuple(outs), in_specs=[SMEM] * len(smem)...]
  transfers between devices with their start and end apart: 58 -> 61, of which waited for: 20 -> 21; matrix products, arithmetic and copies ran while one was open for 6% -> 5% of each run, Pallas kernels for 27% -> 30%
where the time goes in v1:
time: 337 us; the launch traced here: 333 us
  Pallas kernels  108 us (32%)
  waiting for transfers between devices  105 us (31%)
  starting transfers between devices  81.9 us (24%)
  local copies, waits for them, and re-layouts  30.2 us (9%)
  other arithmetic  6.25 us (2%)
    pallas_call x34, Pallas kernels, run(): pl.pallas_call(whole, out_shape=tuple(outs), in_specs=[SMEM] * len(smem)...  108 us
    ppermute x61, waiting for transfers between devices, move(): return lax.ppermute(value, AXES, pairs)  105 us
    ppermute x61, starting transfers between devices, move(): return lax.ppermute(value, AXES, pairs)  81.9 us
    unnamed x121, local copies, waits for them, and re-layouts  17.7 us
  transfers between devices with their start and end apart: 61, of which 21 were waited for; matrix products, arithmetic and copies ran while one was open for 5% of the time, Pallas kernels for 30%

profile of v1, /device:TPU:1, one launch (start us, length us, event | category | flops | bytes accessed | tf_op | source)
XLA Modules:
  0.0 332.8 jit_solution(6907430963210888951)
XLA Ops:
  5.5 5.6 %collective-permute-start.6 = (bf16[96,1536]{1,0:T(8,128)(2,1)S(1)}, bf16[96,1536]{1,0:T(8,128)(2,1)S(1)}, u32[]{:S(2)}, u32[]{:S(2)}) collective-permute-start(bf16[96,1536]{1,0:T(8,128)(2,1)S(1)} %shard_map.247.refs_3_.refs_4_), channel_id=1, source_target_pairs={{2,4},{3,5},{4,2},{5,3},{10,12},{11,13},{12,10},{13,11},{18,20},{1... | collective-permute-start | bytes 884744 | tf_op jit(solution)/shard_map/ppermute | solution.py:134
  15.5 6.0 %constant_dynamic-slice_fusion = bf16[1,1,1500,768]{3,0,2,1:T(2,128)(2,1)S(1)} fusion(bf16[2,1,1500,768]{3,0,2,1:T(2,128)(2,1)} %param.17, s32[]{:T(128)S(6)} %select_n.80), kind=kLoop, calls=%fused_computation.27 | loop fusion | bytes 4608004 | tf_op jit(solution)/shard_map/jit(dynamic_index_in_dim)/dynamic_slice | solution.py:1621
  23.7 6.2 %collective-permute-done.6.refs_3_ = bf16[96,1536]{1,0:T(8,128)(2,1)S(1)} collective-permute-done((bf16[96,1536]{1,0:T(8,128)(2,1)S(1)}, bf16[96,1536]{1,0:T(8,128)(2,1)S(1)}, u32[]{:S(2)}, u32[]{:S(2)}) %collective-permute-start.6) | collective-permute-done | bytes 294944 | tf_op jit(solution)/shard_map/ppermute | solution.py:134
  31.4 6.3 %collective-permute-done.4.refs_1_ = bf16[96,1536]{1,0:T(8,128)(2,1)} collective-permute-done((bf16[96,1536]{1,0:T(8,128)(2,1)S(1)}, bf16[96,1536]{1,0:T(8,128)(2,1)}, u32[]{:S(2)}, u32[]{:S(2)}) %collective-permute-start.4) | collective-permute-done | bytes 294944 | tf_op jit(solution)/shard_map/ppermute | solution.py:134
  50.0 6.8 %collective-permute-done = bf16[224,448]{1,0:T(8,128)(2,1)S(1)} collective-permute-done((bf16[224,448]{1,0:T(8,128)(2,1)S(1)}, bf16[224,448]{1,0:T(8,128)(2,1)S(1)}, u32[]{:S(2)}, u32[]{:S(2)}) %collective-permute-start) | collective-permute-done | bytes 200736 | tf_op jit(solution)/shard_map/ppermute | solution.py:134
  59.8 5.4 %collective-permute-done.8.refs_5_.refs_3_.refs_9_.refs_14_.refs_13_ = bf16[2,2,192,768]{3,2,1,0:T(8,128)(2,1)} collective-permute-done((bf16[2,2,192,768]{3,2,1,0:T(8,128)(2,1)}, bf16[2,2,192,768]{3,2,1,0:T(8,128)(2,1)}, u32[]{:S(2)}, u32[]{:S(2)}) %collective-permute-start.8) | collective-permute-done | bytes 1179680 | tf_op jit(solution)/shard_map/ppermute | solution.py:134
  68.3 5.5 %collective-permute-done.7.refs_4_.refs_2_.refs_8_.refs_13_.refs_12_ = bf16[2,2,192,768]{3,2,1,0:T(8,128)(2,1)} collective-permute-done((bf16[2,2,192,768]{3,2,1,0:T(8,128)(2,1)}, bf16[2,2,192,768]{3,2,1,0:T(8,128)(2,1)}, u32[]{:S(2)}, u32[]{:S(2)}) %collective-permute-start.7) | collective-permute-done | bytes 1179680 | tf_op jit(solution)/shard_map/ppermute | solution.py:134
  78.0 12.1 %collective-permute-done.16.refs_2_ = bf16[192,768]{1,0:T(8,128)(2,1)S(1)} collective-permute-done((bf16[192,768]{1,0:T(8,128)(2,1)S(1)}, bf16[192,768]{1,0:T(8,128)(2,1)S(1)}, u32[]{:S(2)}, u32[]{:S(2)}) %collective-permute-start.16) | collective-permute-done | bytes 294944 | tf_op jit(solution)/shard_map/ppermute | solution.py:134
  96.4 7.6 %shard_map.252 = (bf16[448,768]{1,0:T(8,128)(2,1)S(1)}, bf16[768,448]{1,0:T(8,128)(2,1)S(1)}, bf16[448,1152]{1,0:T(8,128)(2,1)S(1)}, bf16[384,448]{1,0:T(8,128)(...) custom-call(bf16[448,768]{1,0:T(8,128)(2,1)S(1)} %get-tuple-element.107.refs_0_.refs_, ...), custom_call_target="tpu_custom_call" | custom-call | flops 11500000256 | bytes 8886784 | tf_op jit(solution)/shard_map/pallas_call | solution.py:80
  110.5 4.6 %shard_map.253 = (bf16[1536,768]{1,0:T(8,128)(2,1)S(1)}, bf16[768,1536]{1,0:T(8,128)(2,1)S(1)}) custom-call(bf16[1536,768]{1,0:T(8,128)(2,1)S(1)} %pad.4.refs_0_, bf16[2,2,192,768]{3,2,1,0:T(8,128)(2,1)} %shard_map.250.refs_3_.refs_1_.refs_7_.refs_12_.refs_11_, bf16[2,2,192,768]{3,2,1,0:T(8,128)(2,1)} %collective-permute-done.7.refs_4_.refs_2_.refs_8_.refs_13_.refs_12_, ...), custom_call_target="tpu_custom_call" | custom-call | flops 2300000000 | bytes 11796480 | tf_op jit(solution)/shard_map/pallas_call | solution.py:80
  115.2 11.4 %shard_map.254 = (bf16[448,768]{1,0:T(8,128)(2,1)S(1)}, f32[448,768]{1,0:T(8,128)S(1)}, bf16[768,448]{1,0:T(8,128)(2,1)S(1)}, bf16[448,384]{1,0:T(8,128)(2,1)S(1...) custom-call(bf16[448,768]{1,0:T(8,128)(2,1)S(1)} %get-tuple-element.107.refs_0_.refs_1_, ...), custom_call_target="tpu_custom_call" | custom-call | flops 4600000000 | bytes 15325696 | tf_op jit(solution)/shard_map/pallas_call | solution.py:80
  127.3 9.6 %collective-permute-done.18.refs_5_.refs_8_ = bf16[2,2,192,768]{3,2,1,0:T(8,128)(2,1)S(1)} collective-permute-done((bf16[2,2,192,768]{3,2,1,0:T(8,128)(2,1)S(1)}, bf16[2,2,192,768]{3,2,1,0:T(8,128)(2,1)S(1)}, u32[]{:S(2)}, u32[]{:S(2)}) %collective-permute-start.18) | collective-permute-done | bytes 1179680 | tf_op jit(solution)/shard_map/ppermute | solution.py:134
  141.8 7.3 %collective-permute-done.23 = bf16[192,448]{1,0:T(8,128)(2,1)S(1)} collective-permute-done((bf16[192,448]{1,0:T(8,128)(2,1)S(1)}, bf16[192,448]{1,0:T(8,128)(2,1)S(1)}, u32[]{:S(2)}, u32[]{:S(2)}) %collective-permute-start.23) | collective-permute-done | bytes 172064 | tf_op jit(solution)/shard_map/ppermute | solution.py:134
  150.7 5.5 %shard_map.256 = (bf16[448,768]{1,0:T(8,128)(2,1)S(1)}, f32[448,768]{1,0:T(8,128)S(1)}, bf16[768,448]{1,0:T(8,128)(2,1)S(1)}, bf16[448,1536]{1,0:T(8,128)(2,1)S(1)}, bf16[1536,448]{1,0:T(8,128)(2,1)S(1)}) custom-call(f32[448,768]{1,0:T(8,128)S(1)} %get-tuple-element.113.refs_0_.refs_1_, bf16[448,768]{1,0:T(8,128)(2,1)S(1)} %get-tuple-element.114.refs_1_.refs_2_, ...), custom_call_target="tpu_custom_call" | custom-call | flops 10350000128 | bytes 13000704 | tf_op jit(solution)/shard_map/pallas_call | solution.py:80
  161.9 6.0 %shard_map.259 = (bf16[448,768]{1,0:T(8,128)(2,1)S(1)}, f32[448,768]{1,0:T(8,128)S(1)}, bf16[448,768]{1,0:T(8,128)(2,1)S(1)}, bf16[448,1536]{1,0:T(8,128)(2,1)S(...) custom-call(f32[448,768]{1,0:T(8,128)S(1)} %get-tuple-element.116.refs_0_.refs_1_, ...), custom_call_target="tpu_custom_call" | custom-call | flops 11500000256 | bytes 14043136 | tf_op jit(solution)/shard_map/pallas_call | solution.py:80
  172.1 4.4 %shard_map.261 = (bf16[2,4,192,384]{3,2,1,0:T(8,128)(2,1)}, bf16[2,4,192,384]{3,2,1,0:T(8,128)(2,1)S(1)}, bf16[2,4,96,768]{3,2,1,0:T(8,128)(2,1)}, bf16[2,4,96,768]{3,2,1,0:T(8,128)(2,1)S(1)}) custom-call(bf16[768,448]{1,0:T(8,128)(2,1)S(1)} %get-tuple-element.137.refs_0_, bf16[448,1536]{1,0:T(8,128)(2,1)S(1)} %get-tuple-element.138.refs_1_, ...), custom_call_target="tpu_custom_call" | custom-call | flops 6899999744 | bytes 8847360 | tf_op jit(solution)/shard_map/pallas_call | solution.py:80
  179.6 22.1 %shard_map.260 = (bf16[448,768]{1,0:T(8,128)(2,1)S(1)}, f32[448,768]{1,0:T(8,128)S(1)}, bf16[448,768]{1,0:T(8,128)(2,1)S(1)}, bf16[448,384]{1,0:T(8,128)(2,1)S(1...) custom-call(f32[448,768]{1,0:T(8,128)S(1)} %get-tuple-element.124.refs_0_, ...), custom_call_target="tpu_custom_call" | custom-call | flops 25300000768 | bytes 20099584 | tf_op jit(solution)/shard_map/pallas_call | solution.py:80
  226.1 5.2 %collective-permute-done.35.refs_3_.refs_4_ = bf16[2,192,768]{2,1,0:T(8,128)(2,1)S(1)} collective-permute-done((bf16[2,192,768]{2,1,0:T(8,128)(2,1)}, bf16[2,192,768]{2,1,0:T(8,128)(2,1)S(1)}, u32[]{:S(2)}, u32[]{:S(2)}) %collective-permute-start.35) | collective-permute-done | bytes 589856 | tf_op jit(solution)/shard_map/ppermute | solution.py:134
  231.3 4.3 %collective-permute-start.42 = (bf16[192,1500]{1,0:T(8,128)(2,1)S(1)}, bf16[192,1500]{1,0:T(8,128)(2,1)S(1)}, u32[]{:S(2)}, u32[]{:S(2)}) collective-permute-start(bf16[192,1500]{1,0:T(8,128)(2,1)S(1)} %get-tuple-element.158.refs_5_), channel_id=1, source_target_pairs={{0,1},{1,0},{2,5},{3,4},{4,3},{5,2},{6,7},{7,6},{8,9},{9,8},{10,13... | collective-permute-start | bytes 1728008 | tf_op jit(solution)/shard_map/ppermute | solution.py:134
  238.1 5.8 %collective-permute-done.32.refs_2_ = bf16[4,192,384]{2,1,0:T(8,128)(2,1)S(1)} collective-permute-done((bf16[4,192,384]{2,1,0:T(8,128)(2,1)S(1)}, bf16[4,192,384]{2,1,0:T(8,128)(2,1)S(1)}, u32[]{:S(2)}, u32[]{:S(2)}) %collective-permute-start.32) | collective-permute-done | bytes 589856 | tf_op jit(solution)/shard_map/ppermute | solution.py:134
  248.7 11.8 %shard_map.268 = (bf16[448,768]{1,0:T(8,128)(2,1)S(1)}, f32[448,768]{1,0:T(8,128)S(1)}, bf16[448,768]{1,0:T(8,128)(2,1)S(1)}, bf16[448,768]{1,0:T(8,128)(2,1)S(1...) custom-call(f32[448,768]{1,0:T(8,128)S(1)} %copy-done.35, f32[448,768]{1,0:T(8,128)S(1)} %copy-done.29, ...), custom_call_target="tpu_custom_call" | custom-call | flops 13799999488 | bytes 14742016 | tf_op jit(solution)/shard_map/pallas_call | solution.py:80
  260.6 6.2 %collective-permute-done.40.refs_1_ = bf16[2,192,768]{2,1,0:T(8,128)(2,1)S(1)} collective-permute-done((bf16[2,192,768]{2,1,0:T(8,128)(2,1)S(1)}, bf16[2,192,768]{2,1,0:T(8,128)(2,1)S(1)}, u32[]{:S(2)}, u32[]{:S(2)}) %collective-permute-start.40) | collective-permute-done | bytes 589856 | tf_op jit(solution)/shard_map/ppermute | solution.py:134
  279.4 7.8 %collective-permute-done.48.refs_3_.refs_6_ = bf16[2,192,768]{2,1,0:T(8,128)(2,1)S(1)} collective-permute-done((bf16[2,192,768]{2,1,0:T(8,128)(2,1)S(1)}, bf16[2,192,768]{2,1,0:T(8,128)(2,1)S(1)}, u32[]{:S(2)}, u32[]{:S(2)}) %collective-permute-start.48) | collective-permute-done | bytes 589856 | tf_op jit(solution)/shard_map/ppermute | solution.py:134
  325.3 6.4 %collective-permute-done.55.refs_3_ = bf16[112,768]{1,0:T(8,128)(2,1)S(1)} collective-permute-done((bf16[112,768]{1,0:T(8,128)(2,1)S(1)}, bf16[112,768]{1,0:T(8,128)(2,1)S(1)}, u32[]{:S(2)}, u32[]{:S(2)}) %collective-permute-start.55) | collective-permute-done | bytes 172064 | tf_op jit(solution)/shard_map/ppermute | solution.py:134
  (279 shorter events, 150.9 us)
Async XLA Ops:
  5.5 24.4 %collective-permute-start.6 = (bf16[96,1536]{1,0:T(8,128)(2,1)S(1)}, bf16[96,1536]{1,0:T(8,128)(2,1)S(1)}, u32[]{:S(2)}, u32[]{:S(2)}) collective-permute-start(bf16[96,1536]{1,0:T(8,128)(2,1)S(1)} %shard_map.247.refs_3_.refs_4_), channel_id=1, source_target_pairs={{2,4},{3,5},{4,2},{5,3},{10,12},{11,13},{12,10},{13,11},{18,20},{1... | collective-permute-start | bytes 884744 | tf_op jit(solution)/shard_map/ppermute | solution.py:134
  11.2 20.3 %collective-permute-start.5 = (bf16[96,1536]{1,0:T(8,128)(2,1)S(1)}, bf16[96,1536]{1,0:T(8,128)(2,1)S(1)}, u32[]{:S(2)}, u32[]{:S(2)}) collective-permute-start(bf16[96,1536]{1,0:T(8,128)(2,1)S(1)} %shard_map.247.refs_3_.refs_4_), channel_id=1, source_target_pairs={{0,3},{1,2},{2,7},{3,6},{4,1},{5,0},{6,5},{7,4},{8,11},{9,10},{10,... | collective-permute-start | bytes 884744 | tf_op jit(solution)/shard_map/ppermute | solution.py:134
  11.2 26.5 %collective-permute-start.4 = (bf16[96,1536]{1,0:T(8,128)(2,1)S(1)}, bf16[96,1536]{1,0:T(8,128)(2,1)}, u32[]{:S(2)}, u32[]{:S(2)}) collective-permute-start(bf16[96,1536]{1,0:T(8,128)(2,1)S(1)} %shard_map.247.refs_3_.refs_4_), channel_id=1, source_target_pairs={{0,2},{1,3},{2,6},{3,7},{4,0},{5,1},{6,4},{7,5},{8,10},{9,11},{10,... | collective-permute-start | bytes 884744 | tf_op jit(solution)/shard_map/ppermute | solution.py:134
  12.6 25.1 %collective-permute-start.3 = (bf16[96,1536]{1,0:T(8,128)(2,1)S(1)}, bf16[96,1536]{1,0:T(8,128)(2,1)}, u32[]{:S(2)}, u32[]{:S(2)}) collective-permute-start(bf16[96,1536]{1,0:T(8,128)(2,1)S(1)} %shard_map.247.refs_3_.refs_4_), channel_id=1, source_target_pairs={{0,1},{1,0},{2,5},{3,4},{4,3},{5,2},{6,7},{7,6},{8,9},{9,8},{10,13... | collective-permute-start | bytes 884744 | tf_op jit(solution)/shard_map/ppermute | solution.py:134
  15.4 31.3 %collective-permute-start.14 = (bf16[96,384]{1,0:T(8,128)(2,1)S(1)}, bf16[96,384]{1,0:T(8,128)(2,1)}, u32[]{:S(2)}, u32[]{:S(2)}) collective-permute-start(bf16[96,384]{1,0:T(8,128)(2,1)S(1)} %dynamic-slice_bitcast_fusion), channel_id=1, source_target_pairs={{0,4},{1,5},{2,6},{3,7},{4,0},{5,1},{6,2},{7,3},{8,12},{9,13},{10,... | collective-permute-start | bytes 221192 | tf_op jit(solution)/shard_map/ppermute | solution.py:134
  30.0 62.2 %collective-permute-start.11 = (bf16[1500,768]{1,0:T(8,128)(2,1)S(1)}, bf16[1500,768]{1,0:T(8,128)(2,1)}, u32[]{:S(2)}, u32[]{:S(2)}) collective-permute-start(bf16[1500,768]{1,0:T(8,128)(2,1)S(1)} %bitcast.57), channel_id=1, source_target_pairs={{0,4},{1,5},{6,2},{7,3},{8,12},{9,13},{14,10},{15,11},{16,20},{17,... | collective-permute-start | bytes 6912008 | tf_op jit(solution)/shard_map/ppermute | solution.py:134
  40.1 25.1 %collective-permute-start.8 = (bf16[2,2,192,768]{3,2,1,0:T(8,128)(2,1)}, bf16[2,2,192,768]{3,2,1,0:T(8,128)(2,1)}, u32[]{:S(2)}, u32[]{:S(2)}) collective-permute-start(bf16[2,2,192,768]{3,2,1,0:T(8,128)(2,1)} %shard_map.250.refs_3_.refs_1_.refs_7_.refs_12_.refs_11_), channel_id=1, source_target_pairs={{0,16},{1,17},{2,18},{3,19},{4,20},{5,21},{6,22},{7,23},{8,24},{9,... | collective-permute-start | bytes 3538952 | tf_op jit(solution)/shard_map/ppermute | solution.py:134
  45.4 28.4 %collective-permute-start.7 = (bf16[2,2,192,768]{3,2,1,0:T(8,128)(2,1)}, bf16[2,2,192,768]{3,2,1,0:T(8,128)(2,1)}, u32[]{:S(2)}, u32[]{:S(2)}) collective-permute-start(bf16[2,2,192,768]{3,2,1,0:T(8,128)(2,1)} %shard_map.250.refs_3_.refs_1_.refs_7_.refs_12_.refs_11_), channel_id=1, source_target_pairs={{0,8},{1,9},{2,10},{3,11},{4,12},{5,13},{6,14},{7,15},{8,0},{9,1},... | collective-permute-start | bytes 3538952 | tf_op jit(solution)/shard_map/ppermute | solution.py:134
  67.1 23.0 %collective-permute-start.10 = (bf16[2,192,768]{2,1,0:T(8,128)(2,1)}, bf16[2,192,768]{2,1,0:T(8,128)(2,1)}, u32[]{:S(2)}, u32[]{:S(2)}) collective-permute-start(bf16[2,192,768]{2,1,0:T(8,128)(2,1)} %slice_bitcast_fusion.2), channel_id=1, source_target_pairs={{0,8},{1,9},{2,10},{3,11},{4,12},{5,13},{6,14},{7,15},{8,0},{9,1},... | collective-permute-start | bytes 1769480 | tf_op jit(solution)/shard_map/ppermute | solution.py:134
  91.2 35.8 %collective-permute-start.19 = (bf16[2,2,192,768]{3,2,1,0:T(8,128)(2,1)S(1)}, bf16[2,2,192,768]{3,2,1,0:T(8,128)(2,1)S(1)}, u32[]{:S(2)}, u32[]{:S(2)}) collective-permute-start(bf16[2,2,192,768]{3,2,1,0:T(8,128)(2,1)S(1)} %shard_map.255.refs_4_.refs_7_), channel_id=1, source_target_pairs={{0,16},{1,17},{2,18},{3,19},{4,20},{5,21},{6,22},{7,23},{8,24},{9,... | collective-permute-start | bytes 3538952 | tf_op jit(solution)/shard_map/ppermute | solution.py:134
  109.3 27.6 %collective-permute-start.18 = (bf16[2,2,192,768]{3,2,1,0:T(8,128)(2,1)S(1)}, bf16[2,2,192,768]{3,2,1,0:T(8,128)(2,1)S(1)}, u32[]{:S(2)}, u32[]{:S(2)}) collective-permute-start(bf16[2,2,192,768]{3,2,1,0:T(8,128)(2,1)S(1)} %shard_map.255.refs_4_.refs_7_), channel_id=1, source_target_pairs={{0,8},{1,9},{2,10},{3,11},{4,12},{5,13},{6,14},{7,15},{8,0},{9,1},... | collective-permute-start | bytes 3538952 | tf_op jit(solution)/shard_map/ppermute | solution.py:134
  126.6 22.6 %collective-permute-start.13 = (bf16[448,768]{1,0:T(8,128)(2,1)S(1)}, bf16[448,768]{1,0:T(8,128)(2,1)S(1)}, u32[]{:S(2)}, u32[]{:S(2)}) collective-permute-start(bf16[448,768]{1,0:T(8,128)(2,1)S(1)} %get-tuple-element.114.refs_1_.refs_2_), channel_id=1, source_target_pairs={{0,4},{1,5},{2,6},{3,7},{4,0},{5,1},{6,2},{7,3},{8,12},{9,13},{10,... | collective-permute-start | bytes 2064392 | tf_op jit(solution)/shard_map/ppermute | solution.py:134
  127.0 22.6 %collective-permute-start.21 = (bf16[2,192,768]{2,1,0:T(8,128)(2,1)S(1)}, bf16[2,192,768]{2,1,0:T(8,128)(2,1)S(1)}, u32[]{:S(2)}, u32[]{:S(2)}) collective-permute-start(bf16[2,192,768]{2,1,0:T(8,128)(2,1)S(1)} %slice_bitcast_fusion), channel_id=1, source_target_pairs={{0,8},{1,9},{2,10},{3,11},{4,12},{5,13},{6,14},{7,15},{8,0},{9,1},... | collective-permute-start | bytes 1769480 | tf_op jit(solution)/shard_map/ppermute | solution.py:134
  176.5 40.8 %collective-permute-start.30 = (bf16[2,4,192,384]{3,2,1,0:T(8,128)(2,1)}, bf16[2,4,192,384]{3,2,1,0:T(8,128)(2,1)S(1)}, u32[]{:S(2)}, u32[]{:S(2)}) collective-permute-start(bf16[2,4,192,384]{3,2,1,0:T(8,128)(2,1)} %get-tuple-element.142), channel_id=1, source_target_pairs={{0,8},{1,9},{2,10},{3,11},{4,12},{5,13},{6,14},{7,15},{8,0},{9,1},... | collective-permute-start | bytes 3538952 | tf_op jit(solution)/shard_map/ppermute | solution.py:134
  177.7 39.6 %collective-permute-start.31 = (bf16[2,4,96,768]{3,2,1,0:T(8,128)(2,1)}, bf16[2,4,96,768]{3,2,1,0:T(8,128)(2,1)}, u32[]{:S(2)}, u32[]{:S(2)}) collective-permute-start(bf16[2,4,96,768]{3,2,1,0:T(8,128)(2,1)} %get-tuple-element.144), channel_id=1, source_target_pairs={{0,16},{1,17},{2,18},{3,19},{4,20},{5,21},{6,22},{7,23},{8,24},{9,... | collective-permute-start | bytes 3538952 | tf_op jit(solution)/shard_map/ppermute | solution.py:134
  220.4 23.6 %collective-permute-start.32 = (bf16[4,192,384]{2,1,0:T(8,128)(2,1)S(1)}, bf16[4,192,384]{2,1,0:T(8,128)(2,1)S(1)}, u32[]{:S(2)}, u32[]{:S(2)}) collective-permute-start(bf16[4,192,384]{2,1,0:T(8,128)(2,1)S(1)} %get-tuple-element.151.refs_2_), channel_id=1, source_target_pairs={{0,16},{1,17},{2,18},{3,19},{4,20},{5,21},{6,22},{7,23},{8,24},{9,... | collective-permute-start | bytes 1769480 | tf_op jit(solution)/shard_map/ppermute | solution.py:134
  221.7 22.4 %collective-permute-start.33 = (bf16[4,96,768]{2,1,0:T(8,128)(2,1)S(1)}, bf16[4,96,768]{2,1,0:T(8,128)(2,1)S(1)}, u32[]{:S(2)}, u32[]{:S(2)}) collective-permute-start(bf16[4,96,768]{2,1,0:T(8,128)(2,1)S(1)} %get-tuple-element.152.refs_3_), channel_id=1, source_target_pairs={{0,8},{1,9},{2,10},{3,11},{4,12},{5,13},{6,14},{7,15},{8,0},{9,1},... | collective-permute-start | bytes 1769480 | tf_op jit(solution)/shard_map/ppermute | solution.py:134
  222.0 25.3 %collective-permute-start.29 = (bf16[448,768]{1,0:T(8,128)(2,1)S(1)}, bf16[448,768]{1,0:T(8,128)(2,1)S(1)}, u32[]{:S(2)}, u32[]{:S(2)}) collective-permute-start(bf16[448,768]{1,0:T(8,128)(2,1)S(1)} %copy-done.9), channel_id=1, source_target_pairs={{0,4},{1,5},{2,6},{3,7},{4,0},{5,1},{6,2},{7,3},{8,12},{9,13},{10,... | collective-permute-start | bytes 2064392 | tf_op jit(solution)/shard_map/ppermute | solution.py:134
  231.3 42.6 %collective-permute-start.42 = (bf16[192,1500]{1,0:T(8,128)(2,1)S(1)}, bf16[192,1500]{1,0:T(8,128)(2,1)S(1)}, u32[]{:S(2)}, u32[]{:S(2)}) collective-permute-start(bf16[192,1500]{1,0:T(8,128)(2,1)S(1)} %get-tuple-element.158.refs_5_), channel_id=1, source_target_pairs={{0,1},{1,0},{2,5},{3,4},{4,3},{5,2},{6,7},{7,6},{8,9},{9,8},{10,13... | collective-permute-start | bytes 1728008 | tf_op jit(solution)/shard_map/ppermute | solution.py:134
  235.6 38.3 %collective-permute-start.41 = (bf16[192,1500]{1,0:T(8,128)(2,1)S(1)}, bf16[192,1500]{1,0:T(8,128)(2,1)S(1)}, u32[]{:S(2)}, u32[]{:S(2)}) collective-permute-start(bf16[192,1500]{1,0:T(8,128)(2,1)S(1)} %get-tuple-element.157.refs_4_.refs_0_), channel_id=1, source_target_pairs={{2,4},{3,5},{4,2},{5,3},{10,12},{11,13},{12,10},{13,11},{18,20},{1... | collective-permute-start | bytes 1728008 | tf_op jit(solution)/shard_map/ppermute | solution.py:134
  243.9 27.6 %collective-permute-start.38 = (bf16[192,768]{1,0:T(8,128)(2,1)S(1)}, bf16[192,768]{1,0:T(8,128)(2,1)S(1)}, u32[]{:S(2)}, u32[]{:S(2)}) collective-permute-start(bf16[192,768]{1,0:T(8,128)(2,1)S(1)} %get-tuple-element.159.refs_6_), channel_id=1, source_target_pairs={{0,16},{1,17},{2,18},{3,19},{4,20},{5,21},{6,22},{7,23},{8,24},{9,... | collective-permute-start | bytes 884744 | tf_op jit(solution)/shard_map/ppermute | solution.py:134
  244.2 28.3 %collective-permute-start.39 = (bf16[192,768]{1,0:T(8,128)(2,1)S(1)}, bf16[192,768]{1,0:T(8,128)(2,1)S(1)}, u32[]{:S(2)}, u32[]{:S(2)}) collective-permute-start(bf16[192,768]{1,0:T(8,128)(2,1)S(1)} %get-tuple-element.160.refs_7_), channel_id=1, source_target_pairs={{0,8},{1,9},{2,10},{3,11},{4,12},{5,13},{6,14},{7,15},{8,0},{9,1},... | collective-permute-start | bytes 884744 | tf_op jit(solution)/shard_map/ppermute | solution.py:134
  274.7 24.0 %collective-permute-start.57 = (bf16[96,768]{1,0:T(8,128)(2,1)S(1)}, bf16[96,768]{1,0:T(8,128)(2,1)S(1)}, u32[]{:S(2)}, u32[]{:S(2)}) collective-permute-start(bf16[96,768]{1,0:T(8,128)(2,1)S(1)} %get-tuple-element.188), channel_id=1, source_target_pairs={{0,4},{1,5},{2,0},{3,1},{4,6},{5,7},{6,2},{7,3},{8,12},{9,13},{10,... | collective-permute-start | bytes 442376 | tf_op jit(solution)/shard_map/ppermute | solution.py:134
  303.4 20.9 %collective-permute-start.43 = (bf16[192,448]{1,0:T(8,128)(2,1)S(1)}, bf16[192,448]{1,0:T(8,128)(2,1)S(1)}, u32[]{:S(2)}, u32[]{:S(2)}) collective-permute-start(bf16[192,448]{1,0:T(8,128)(2,1)S(1)} %get-tuple-element.173.refs_0_), channel_id=1, source_target_pairs={{2,4},{3,5},{4,2},{5,3},{10,12},{11,13},{12,10},{13,11},{18,20},{1... | collective-permute-start | bytes 516104 | tf_op jit(solution)/shard_map/ppermute | solution.py:134
  (97 other events, 1009.3 us)
